TPU v7x, 32 devices: a whole 2x2x4 slice. The times are simulated.
32 devices in a mesh: dp: 8 (over z, x), blk: 4 (over y, core).
Axes of the slice: x: 2, y: 2, z: 4, core: 2. Of those that a mesh axis runs over, the one named last changes fastest.
Arguments:
- patches: bfloat16 [32768, 768], P(('dp', 'blk')), may hold values from -6 to 6
- cotangent: bfloat16 [32768, 768], P(('dp', 'blk')), may hold values from -6 to 6
- short_lengths: int32 [32, 9], P(('dp', 'blk')), may hold values from 1 to 128, 896 in all within a row
- long_lengths: int32 [8], P('dp'), may hold values from 385 to 512, as said below
- w_qkv: float32 [768, 2304], P(('dp', 'blk')), may hold values from -0.21875 to 0.21875
- w_out: float32 [768, 768], P(('dp', 'blk')), may hold values from -0.625 to 0.625
- w_up: float32 [768, 3072], P(('dp', 'blk')), may hold values from -0.21875 to 0.21875
- w_down: float32 [3072, 768], P(('dp', 'blk')), may hold values from -0.109375 to 0.109375
- vectors: float32 [12, 768], P(None, ('dp', 'blk'))
- first_qkv: float32 [768, 2304], P(('dp', 'blk')), may hold values from -0.0024414062 to 0.0024414062
- first_out: float32 [768, 768], P(('dp', 'blk')), may hold values from -0.0024414062 to 0.0024414062
- first_up: float32 [768, 3072], P(('dp', 'blk')), may hold values from -0.0024414062 to 0.0024414062
- first_down: float32 [3072, 768], P(('dp', 'blk')), may hold values from -0.0024414062 to 0.0024414062
- first_vectors: float32 [12, 768], P(None, ('dp', 'blk')), may hold values from -0.0034179688 to 0.0034179688
- second_qkv: float32 [768, 2304], P(('dp', 'blk')), may hold values from 1.4128508e-07 to 5.6514034e-07
- second_out: float32 [768, 768], P(('dp', 'blk')), may hold values from 1.4128508e-07 to 5.6514034e-07
- second_up: float32 [768, 3072], P(('dp', 'blk')), may hold values from 1.4128508e-07 to 5.6514034e-07
- second_down: float32 [3072, 768], P(('dp', 'blk')), may hold values from 1.4128508e-07 to 5.6514034e-07
- second_vectors: float32 [12, 768], P(None, ('dp', 'blk')), may hold values from 2.8257017e-07 to 1.1302807e-06
Outputs:
- output: bfloat16 [32768, 768], P(('dp', 'blk'))
- input_grad: float32 [32768, 768], P(('dp', 'blk'))
- grad_norm: float32 [], replicated
- new_qkv: float32 [768, 2304], P(('dp', 'blk'))
- new_out: float32 [768, 768], P(('dp', 'blk'))
- new_up: float32 [768, 3072], P(('dp', 'blk'))
- new_down: float32 [3072, 768], P(('dp', 'blk'))
- new_vectors: float32 [12, 768], P(None, ('dp', 'blk'))
- new_first_qkv: float32 [768, 2304], P(('dp', 'blk'))
- new_first_out: float32 [768, 768], P(('dp', 'blk'))
- new_first_up: float32 [768, 3072], P(('dp', 'blk'))
- new_first_down: float32 [3072, 768], P(('dp', 'blk'))
- new_first_vectors: float32 [12, 768], P(None, ('dp', 'blk'))
- new_second_qkv: float32 [768, 2304], P(('dp', 'blk'))
- new_second_out: float32 [768, 768], P(('dp', 'blk'))
- new_second_up: float32 [768, 3072], P(('dp', 'blk'))
- new_second_down: float32 [3072, 768], P(('dp', 'blk'))
- new_second_vectors: float32 [12, 768], P(None, ('dp', 'blk'))
- copy_qkv: bfloat16 [768, 2304], P(('dp', 'blk'))
- copy_out: bfloat16 [768, 768], P(('dp', 'blk'))
- copy_up: bfloat16 [768, 3072], P(('dp', 'blk'))
- copy_down: bfloat16 [3072, 768], P(('dp', 'blk'))
- copy_vectors: bfloat16 [12, 768], P(None, ('dp', 'blk'))
Inputs may be any that keep to these rules, and one draw needn't show every extreme that they name: `short_lengths`: each row holds the lengths of the 9 short clips packed in order into one device's 896 short rows; it sums to 896 and its largest entry is 128. `long_lengths`: the long clip of each index of dp spans its 4 devices along blk in order; some index has 512.
All inputs are finite; a program needn't handle non-finite values.
Results may differ from a plain program's by a relative error of at most 0.012.
The roundings to bfloat16 on the way count: a program that leaves them out, or rounds other values in their place, can miss the bound.
Values may be sent and summed in bfloat16 or wider, within the bound.
A program may use at most 256 MiB of HBM per device.

v0:
```python
import jax
import jax.numpy as jnp
from jax import lax
from jax.sharding import PartitionSpec as P

HD = 64
SHORT_DEV = 896
LONG_DEV = 128
STEP = 10


eps_norm = 1e-06
far_below = -1000000000.0
rate_matrix = 0.04
rate_vector = 0.5
beta_first = 0.5
beta_second = 0.5
eps_adam = 1e-08
decay_weight = 0.01


def times_transposed(left_side, right_side):
    return lax.dot_general(
        left_side, right_side, (((1,), (1,)), ((), ())), preferred_element_type=jnp.float32
    )


def outer_sum(left_side, right_side):
    return lax.dot_general(
        left_side, right_side, (((0,), (0,)), ((), ())), preferred_element_type=jnp.float32
    )


def normalize(values, gain, shift):
    row_mean = jnp.mean(values, -1, keepdims=True)
    centered = values - row_mean
    inv_std = lax.rsqrt(jnp.mean(centered * centered, -1, keepdims=True) + eps_norm)
    standard = centered * inv_std
    return (standard, inv_std, standard * gain + shift)


def norm_back(upstream, standard, inv_std, gain):
    scaled = upstream * gain
    inner = (
        scaled
        - jnp.mean(scaled, -1, keepdims=True)
        - standard * jnp.mean(scaled * standard, -1, keepdims=True)
    )
    return (inner * inv_std, jnp.sum(upstream * standard, 0), jnp.sum(upstream, 0))


def masked_scores(queries, key_rows, allowed):
    raw_scores = jnp.einsum(
        "qhd,khd->hqk", queries, key_rows, preferred_element_type=jnp.float32
    ) * HD ** (-0.5)
    return jnp.where(allowed[None], raw_scores, far_below)


def attend_forward(queries, key_rows, value_rows, allowed):
    scores = masked_scores(queries, key_rows, allowed)
    row_top = jnp.max(scores, -1, keepdims=True)
    exponent = jnp.exp(scores - row_top)
    row_total = jnp.sum(exponent, -1, keepdims=True)
    attn_probs = (exponent / row_total).astype(jnp.bfloat16)
    attn_out = jnp.einsum(
        "hqk,khd->qhd", attn_probs, value_rows, preferred_element_type=jnp.float32
    )
    return (attn_out.reshape(attn_out.shape[0], -1), row_top + jnp.log(row_total))


def attend_back(queries, key_rows, value_rows, allowed, log_total, upstream):
    scores = masked_scores(queries, key_rows, allowed)
    attn_probs = jnp.exp(scores - log_total)
    grad_probs = jnp.einsum(
        "qhd,khd->hqk", upstream, value_rows, preferred_element_type=jnp.float32
    )
    row_delta = jnp.sum(attn_probs * grad_probs, -1, keepdims=True)
    grad_scores = (attn_probs * (grad_probs - row_delta)).astype(jnp.bfloat16)
    score_scale = HD ** (-0.5)
    grad_query = (
        jnp.einsum("hqk,khd->qhd", grad_scores, key_rows, preferred_element_type=jnp.float32)
        * score_scale
    )
    grad_key = (
        jnp.einsum("hqk,qhd->khd", grad_scores, queries, preferred_element_type=jnp.float32)
        * score_scale
    )
    grad_value = jnp.einsum(
        "hqk,qhd->khd",
        attn_probs.astype(jnp.bfloat16),
        upstream,
        preferred_element_type=jnp.float32,
    )
    return (
        grad_query.reshape(grad_query.shape[0], -1),
        grad_key.reshape(grad_key.shape[0], -1),
        grad_value.reshape(grad_value.shape[0], -1),
    )


def adamw_step(weight, gradient, first_moment, second_moment, rate, decay):
    first_new = beta_first * first_moment + (1.0 - beta_first) * gradient
    second_new = beta_second * second_moment + (1.0 - beta_second) * gradient * gradient
    first_hat = first_new / (1.0 - beta_first**STEP)
    second_hat = second_new / (1.0 - beta_second**STEP)
    weight_new = weight - rate * (first_hat / (jnp.sqrt(second_hat) + eps_adam) + decay * weight)
    return (weight_new, first_new, second_new)


def per_device(
    patches,
    cotangent,
    short_lengths,
    long_lengths,
    w_qkv,
    w_out,
    w_up,
    w_down,
    vectors,
    first_qkv,
    first_out,
    first_up,
    first_down,
    first_vectors,
    second_qkv,
    second_out,
    second_up,
    second_down,
    second_vectors,
):
    low_qkv = w_qkv.astype(jnp.bfloat16)
    low_out = w_out.astype(jnp.bfloat16)
    low_up = w_up.astype(jnp.bfloat16)
    low_down = w_down.astype(jnp.bfloat16)
    low_vec = vectors.astype(jnp.bfloat16)
    full_qkv, full_out, full_up, full_down, full_vec = (
        lax.all_gather(low_qkv, ("dp", "blk"), axis=0, tiled=True),
        lax.all_gather(low_out, ("dp", "blk"), axis=0, tiled=True),
        lax.all_gather(low_up, ("dp", "blk"), axis=0, tiled=True),
        lax.all_gather(low_down, ("dp", "blk"), axis=0, tiled=True),
        lax.all_gather(low_vec, ("dp", "blk"), axis=1, tiled=True),
    )
    params = full_vec.astype(jnp.float32)
    gain_one, shift_one, gain_two, shift_two = (params[0], params[1], params[2], params[3])
    bias_qkv = jnp.concatenate([params[4], jnp.zeros_like(params[4]), params[5]])
    bias_out, bias_down = (params[6], params[7])
    bias_up = params[8:12].reshape(-1)
    model_width = patches.shape[1]
    head_count = model_width // HD
    inputs = patches.astype(jnp.float32)
    unit_one, inv_one, normed_one = normalize(inputs, gain_one, shift_one)
    hidden_one = normed_one.astype(jnp.bfloat16)
    projected = (
        jnp.dot(hidden_one, full_qkv, preferred_element_type=jnp.float32) + bias_qkv
    ).astype(jnp.bfloat16)
    query_part = projected[:, :model_width]
    key_part = projected[:, model_width : 2 * model_width]
    value_part = projected[:, 2 * model_width :]
    queries = query_part.reshape(-1, head_count, HD)
    seg_ends = jnp.cumsum(short_lengths[0])
    positions = jnp.arange(SHORT_DEV, dtype=jnp.int32)
    segment_ids = jnp.sum((positions[:, None] >= seg_ends[None, :]).astype(jnp.int32), 1)
    short_allowed = segment_ids[:, None] == segment_ids[None, :]
    short_keys = key_part[:SHORT_DEV].reshape(-1, head_count, HD)
    short_values = value_part[:SHORT_DEV].reshape(-1, head_count, HD)
    far_keys, far_values = (
        lax.all_gather(key_part[SHORT_DEV:], "blk", axis=0, tiled=True),
        lax.all_gather(value_part[SHORT_DEV:], "blk", axis=0, tiled=True),
    )
    far_keys = far_keys.reshape(-1, head_count, HD)
    far_values = far_values.reshape(-1, head_count, HD)
    length = long_lengths[0]
    key_ok = jnp.arange(far_keys.shape[0], dtype=jnp.int32) < length
    long_allowed = jnp.broadcast_to(key_ok[None, :], (LONG_DEV, far_keys.shape[0]))
    short_out, short_lse = attend_forward(
        queries[:SHORT_DEV], short_keys, short_values, short_allowed
    )
    long_out, long_lse = attend_forward(queries[SHORT_DEV:], far_keys, far_values, long_allowed)
    attended = jnp.concatenate([short_out, long_out], 0).astype(jnp.bfloat16)
    middle = inputs + (jnp.dot(attended, full_out, preferred_element_type=jnp.float32) + bias_out)
    unit_two, inv_two, normed_two = normalize(middle, gain_two, shift_two)
    hidden_two = normed_two.astype(jnp.bfloat16)
    pre_act = jnp.dot(hidden_two, full_up, preferred_element_type=jnp.float32) + bias_up
    activated, gelu_back = jax.vjp(jax.nn.gelu, pre_act)
    act_low = activated.astype(jnp.bfloat16)
    result = middle + (jnp.dot(act_low, full_down, preferred_element_type=jnp.float32) + bias_down)
    back_qkv, back_out, back_up, back_down, back_vec = (
        full_qkv,
        full_out,
        full_up,
        full_down,
        full_vec,
    )
    back_params = back_vec.astype(jnp.float32)
    long_place = lax.axis_index("blk") * LONG_DEV + jnp.arange(LONG_DEV, dtype=jnp.int32)
    row_keep = jnp.concatenate(
        [jnp.ones((SHORT_DEV,), jnp.float32), (long_place < length).astype(jnp.float32)]
    )
    grad_result = cotangent.astype(jnp.float32) * row_keep[:, None]
    grad_low = grad_result.astype(jnp.bfloat16)
    grad_down = outer_sum(act_low, grad_low)
    sum_down = jnp.sum(grad_low, 0, dtype=jnp.float32)
    grad_act = times_transposed(grad_low, back_down)
    grad_pre = gelu_back(grad_act)[0].astype(jnp.bfloat16)
    grad_up = outer_sum(hidden_two, grad_pre)
    sum_up = jnp.sum(grad_pre, 0, dtype=jnp.float32)
    grad_hidden_two = times_transposed(grad_pre, back_up)
    back_mid, gain_two_grad, shift_two_grad = norm_back(
        grad_hidden_two, unit_two, inv_two, back_params[2]
    )
    grad_middle = grad_result + back_mid
    grad_branch = grad_middle.astype(jnp.bfloat16)
    grad_out = outer_sum(attended, grad_branch)
    sum_out = jnp.sum(grad_branch, 0, dtype=jnp.float32)
    grad_att = (
        times_transposed(grad_branch, back_out).astype(jnp.bfloat16).reshape(-1, head_count, HD)
    )
    short_dq, short_dk, short_dv = attend_back(
        queries[:SHORT_DEV],
        short_keys,
        short_values,
        short_allowed,
        short_lse,
        grad_att[:SHORT_DEV],
    )
    long_dq, long_dk, long_dv = attend_back(
        queries[SHORT_DEV:], far_keys, far_values, long_allowed, long_lse, grad_att[SHORT_DEV:]
    )
    near_dk, near_dv = (
        lax.psum_scatter(
            long_dk.astype(jnp.bfloat16), "blk", scatter_dimension=0, tiled=True
        ).astype(jnp.float32),
        lax.psum_scatter(
            long_dv.astype(jnp.bfloat16), "blk", scatter_dimension=0, tiled=True
        ).astype(jnp.float32),
    )
    grad_mixed = jnp.concatenate(
        [
            jnp.concatenate([short_dq, short_dk, short_dv], 1),
            jnp.concatenate([long_dq, near_dk, near_dv], 1),
        ],
        0,
    ).astype(jnp.bfloat16)
    grad_qkv = outer_sum(hidden_one, grad_mixed)
    sums_mixed = jnp.sum(grad_mixed, 0, dtype=jnp.float32)
    grad_hidden_one = times_transposed(grad_mixed, back_qkv)
    back_in, gain_one_grad, shift_one_grad = norm_back(
        grad_hidden_one, unit_one, inv_one, back_params[0]
    )
    input_grad = grad_middle + back_in
    grad_vec = jnp.concatenate(
        [
            jnp.stack(
                [
                    gain_one_grad,
                    shift_one_grad,
                    gain_two_grad,
                    shift_two_grad,
                    sums_mixed[:model_width],
                    sums_mixed[2 * model_width :],
                    sum_out,
                    sum_down,
                ]
            ),
            sum_up.reshape(-1, model_width),
        ],
        0,
    )
    red_qkv, red_out, red_up, red_down, red_vec = (
        lax.psum_scatter(grad_qkv, ("dp", "blk"), scatter_dimension=0, tiled=True),
        lax.psum_scatter(grad_out, ("dp", "blk"), scatter_dimension=0, tiled=True),
        lax.psum_scatter(grad_up, ("dp", "blk"), scatter_dimension=0, tiled=True),
        lax.psum_scatter(grad_down, ("dp", "blk"), scatter_dimension=0, tiled=True),
        lax.psum_scatter(grad_vec, ("dp", "blk"), scatter_dimension=1, tiled=True),
    )
    local_square = (
        jnp.sum(red_qkv * red_qkv)
        + jnp.sum(red_out * red_out)
        + jnp.sum(red_up * red_up)
        + jnp.sum(red_down * red_down)
        + jnp.sum(red_vec * red_vec)
    )
    square_sum = lax.psum(local_square, ("dp", "blk"))
    grad_norm = jnp.sqrt(square_sum)
    clip_factor = 1.0 / jnp.maximum(grad_norm, 1.0)
    qkv_new = adamw_step(
        w_qkv, red_qkv * clip_factor, first_qkv, second_qkv, rate_matrix, decay_weight
    )
    out_new = adamw_step(
        w_out, red_out * clip_factor, first_out, second_out, rate_matrix, decay_weight
    )
    up_new = adamw_step(w_up, red_up * clip_factor, first_up, second_up, rate_matrix, decay_weight)
    down_new = adamw_step(
        w_down, red_down * clip_factor, first_down, second_down, rate_matrix, decay_weight
    )
    vec_new = adamw_step(
        vectors, red_vec * clip_factor, first_vectors, second_vectors, rate_vector, 0.0
    )
    return (
        result.astype(jnp.bfloat16),
        input_grad,
        grad_norm,
        qkv_new[0],
        out_new[0],
        up_new[0],
        down_new[0],
        vec_new[0],
        qkv_new[1],
        out_new[1],
        up_new[1],
        down_new[1],
        vec_new[1],
        qkv_new[2],
        out_new[2],
        up_new[2],
        down_new[2],
        vec_new[2],
        qkv_new[0].astype(jnp.bfloat16),
        out_new[0].astype(jnp.bfloat16),
        up_new[0].astype(jnp.bfloat16),
        down_new[0].astype(jnp.bfloat16),
        vec_new[0].astype(jnp.bfloat16),
    )


def solution(mesh):
    placed = (
        P(("dp", "blk"), None),
        P(("dp", "blk"), None),
        P(("dp", "blk"), None),
        P("dp"),
        P(("dp", "blk"), None),
        P(("dp", "blk"), None),
        P(("dp", "blk"), None),
        P(("dp", "blk"), None),
        P(None, ("dp", "blk")),
        P(("dp", "blk"), None),
        P(("dp", "blk"), None),
        P(("dp", "blk"), None),
        P(("dp", "blk"), None),
        P(None, ("dp", "blk")),
        P(("dp", "blk"), None),
        P(("dp", "blk"), None),
        P(("dp", "blk"), None),
        P(("dp", "blk"), None),
        P(None, ("dp", "blk")),
    )
    return jax.shard_map(
        per_device,
        mesh=mesh,
        in_specs=placed,
        out_specs=(
            P(("dp", "blk"), None),
            P(("dp", "blk"), None),
            P(),
            P(("dp", "blk"), None),
            P(("dp", "blk"), None),
            P(("dp", "blk"), None),
            P(("dp", "blk"), None),
            P(None, ("dp", "blk")),
            P(("dp", "blk"), None),
            P(("dp", "blk"), None),
            P(("dp", "blk"), None),
            P(("dp", "blk"), None),
            P(None, ("dp", "blk")),
            P(("dp", "blk"), None),
            P(("dp", "blk"), None),
            P(("dp", "blk"), None),
            P(("dp", "blk"), None),
            P(None, ("dp", "blk")),
            P(("dp", "blk"), None),
            P(("dp", "blk"), None),
            P(("dp", "blk"), None),
            P(("dp", "blk"), None),
            P(None, ("dp", "blk")),
        ),
        check_vma=False,
    )
```

profile of v0, /device:TPU:0, one launch (start us, length us, event | category | flops | bytes accessed | tf_op | source)
XLA Modules:
  0.0 974.2 jit_solution(68056338780703145)
XLA Ops:
  14.6 43.7 %all-gather = bf16[32,24,12]{1,2,0:T(8,128)(2,1)S(1)} all-gather(bf16[1,24,12]{1,2,0:T(8,128)(2,1)S(1)} %convert_bitcast_fusion), channel_id=1, replica_groups=mesh['dp'=8,'blk'=4] {'dp','blk'}, dimensions={0}, use_global_device_ids=true | all-gather | bytes 19008 | tf_op jit(solution)/shard_map/all_gather | solution.py:141
  65.7 2.6 copy.138
  68.3 6.2 all-gather.6.cloned.1.call-done
  74.6 6.4 add_convert_fusion
  84.5 2.0 copy.135
  86.5 8.8 all_gather.24
  96.5 9.4 all_gather.23
  107.1 2.0 copy.131
  109.2 3.0 copy.130
  117.0 15.8 %fusion.75 = (f32[12,896]{1,0:T(8,128)S(1)}, f32[12,896,896]{1,2,0:T(8,128)}) fusion(bf16[896,12,64]{0,2,1:T(8,128)(2,1)S(1)} %bitcast.82, bf16[896,12,64]{0,2,1:T(8,128)(2,1)S(1)} %bitcast.84, pred[896,896]{0,1:T(8,128)(4,1)S(1)} %broadcast_compare_fusion), kind=kOutput, calls=%fused_computation.146 | convolution fusion | flops 1262016000 | bytes 42133504 | tf_op jit(solution)/shard_map/qhd,khd->hqk/dot_general | solution.py:53
  132.7 15.2 %fusion = f32[12,896]{1,0:T(8,128)S(1)} fusion(f32[12,896,896]{1,2,0:T(8,128)} %get-tuple-element.188, f32[12,896]{1,0:T(8,128)S(1)} %get-tuple-element.187), kind=kLoop, calls=%fused_computation.6 | loop fusion | flops 19256832 | bytes 38621184 | tf_op jit(solution)/shard_map/reduce_sum | solution.py:63
  147.9 16.7 %fusion.33 = bf16[12,64,896]{2,1,0:T(8,128)(2,1)} fusion(bf16[896,12,64]{0,2,1:T(8,128)(2,1)S(1)} %bitcast.89, f32[12,896,896]{1,2,0:T(8,128)} %get-tuple-element.188, f32[12,896]{1,0:T(8,128)S(1)} %fusion, f32[12,896]{1,0:T(8,128)} %copy-done.29), kind=kOutput, calls=%fused_computation.67 | convolution fusion | flops 1262714880 | bytes 41373696 | tf_op jit(solution)/shard_map/hqk,khd->qhd/dot_general | solution.py:65
  164.6 3.8 fusion.76
  169.4 27.6 %all-gather.10.cloned.1.call-done = bf16[768,3072]{1,0:T(8,128)(2,1)} async-done(((bf16[24,3072]{1,0:T(8,128)(2,1)}), bf16[768,3072]{1,0:T(8,128)(2,1)}) %all-gather.10.cloned.1.call-update) | async-done | bytes 4718608 | tf_op jit(solution)/shard_map/all_gather | solution.py:139
  197.0 11.1 %fusion.60 = f32[1024,3072]{1,0:T(8,128)} fusion(bf16[768,3072]{1,0:T(8,128)(2,1)} %all-gather.10.cloned.1.call-done, f32[1024,768]{0,1:T(8,128)S(1)} %get-tuple-element.190, f32[768]{0:T(1024)S(1)} %copy-done.32, f32[768]{0:T(1024)S(1)} %copy-done.31, f32[1024]{0:T(1024)S(1)} %add_rsqrt_fusion, f32[1024]{0:T(1024)S(1)} %broadcast_multiply_fusion.4), kind=kOutput, calls=%fused_computation.136 | convolution fusion | flops 4835770368 | bytes 20461568 | tf_op jit(solution)/shard_map/dot_general | solution.py:183
  208.1 54.7 %all-gather.12.cloned.1.call-done = bf16[3072,768]{1,0:T(8,128)(2,1)} async-done(((bf16[96,768]{1,0:T(8,128)(2,1)}), bf16[3072,768]{1,0:T(8,128)(2,1)}) %all-gather.12.cloned.1.call-update) | async-done | bytes 4718608 | tf_op jit(solution)/shard_map/all_gather | solution.py:140
  262.8 17.4 %convert_reduce_fusion = (f32[3072]{0:T(1024)}, bf16[1024,3072]{1,0:T(8,128)(2,1)S(1)}) fusion(f32[1024,3072]{1,0:T(8,128)} %fusion.60, f32[3072]{0:T(1024)S(1)} %copy-done.58, bf16[3072,768]{1,0:T(8,128)(2,1)} %all-gather.12.cloned.1.call-done, bf16[1024,768]{0,1:T(8,128)(2,1)} %copy.138, f32[1024]{0:T(1024)S(1)} %copy-done.57), kind=kOutput, calls=%fused_computation.20 | convolution fusion | flops 4906546176 | bytes 25194496 | tf_op jit(solution)/shard_map/dot_general | solution.py:23
  280.2 7.3 fusion.78
  287.5 3.6 copy.139
  291.1 3.6 multiply_reduce_fusion.1
  294.7 2.3 convert_reduce_fusion.4
  300.1 16.2 %fusion.30 = bf16[12,64,896]{2,1,0:T(8,128)(2,1)} fusion(bf16[896,12,64]{0,2,1:T(8,128)(2,1)S(1)} %bitcast.80, f32[12,896,896]{1,2,0:T(8,128)} %get-tuple-element.188, f32[12,896]{1,0:T(8,128)S(1)} %log_add_fusion), kind=kOutput, calls=%fused_computation.66 | convolution fusion | flops 1253081088 | bytes 41330688 | tf_op jit(solution)/shard_map/hqk,qhd->khd/dot_general | solution.py:88
  316.3 29.9 %multiply_reduce_fusion = (f32[12,896]{1,0:T(8,128)S(1)}, f32[12,896,896]{1,2,0:T(8,128)}) fusion(f32[12,896,896]{1,2,0:T(8,128)} %get-tuple-element.188, f32[12,896]{1,0:T(8,128)S(1)} %log_add_fusion, bf16[896,12,64]{0,2,1:T(8,128)(2,1)} %bitcast.81, bf16[896,12,64]{0,2,1:T(8,128)(2,1)} %bitcast.88), kind=kOutput, calls=%fused_computation.1 | convolution fusion | flops 1262016000 | bytes 79908864 | tf_op jit(solution)/shard_map/qhd,khd->hqk/dot_general | solution.py:74
  347.9 2.3 copy.155
  350.2 2.2 multiply_reduce_fusion.2
  355.7 2.5 copy.153
  358.2 2.3 fusion.44
  360.5 4.3 fusion.46
  364.8 31.5 %multiply_convert_fusion = bf16[12,896,896]{1,2,0:T(8,128)(2,1)} fusion(f32[12,896,896]{1,2,0:T(8,128)} %get-tuple-element.194, f32[12,896,896]{1,2,0:T(8,128)} %get-tuple-element.188, f32[12,896]{1,0:T(8,128)S(1)} %get-tuple-element.193, f32[12,896]{1,0:T(8,128)S(1)} %log_add_fusion), kind=kLoop, calls=%fused_computation | loop fusion | flops 38535168 | bytes 96423936 | tf_op jit(solution)/shard_map/convert_element_type | solution.py:78
  396.4 10.8 %multiply_convert_fusion.3 = bf16[12,64,896]{2,1,0:T(8,128)(2,1)} fusion(bf16[896,12,64]{0,2,1:T(8,128)(2,1)S(1)} %bitcast.83, bf16[12,896,896]{1,2,0:T(8,128)(2,1)} %multiply_convert_fusion), kind=kOutput, calls=%fused_computation.62 | convolution fusion | flops 1234501632 | bytes 22020096 | tf_op jit(solution)/shard_map/hqk,qhd->khd/dot_general | solution.py:85
  408.6 10.9 %multiply_convert_fusion.4 = bf16[12,64,896]{2,1,0:T(8,128)(2,1)} fusion(bf16[896,12,64]{0,2,1:T(8,128)(2,1)S(1)} %bitcast.85, bf16[12,896,896]{1,2,0:T(8,128)(2,1)} %multiply_convert_fusion), kind=kOutput, calls=%fused_computation.63 | convolution fusion | flops 1234501632 | bytes 22020096 | tf_op jit(solution)/shard_map/hqk,khd->qhd/dot_general | solution.py:81
  421.8 9.4 convert_reduce_fusion.1
  431.2 2.3 copy-done.20
  433.5 6.4 fusion.56
  441.8 10.6 %fusion.59 = f32[768,3072]{1,0:T(8,128)} fusion(bf16[1024,3072]{1,0:T(8,128)(2,1)} %copy-done.70, f32[1024,768]{0,1:T(8,128)S(1)} %copy-done.3, f32[768]{0:T(1024)S(1)} %copy-done.33, f32[768]{0:T(1024)S(1)} %copy-done.31, f32[1024]{0:T(1024)S(1)} %add_rsqrt_fusion, f32[1024]{0:T(1024)S(1)} %broadcast_multiply_fusion.4), kind=kOutput, calls=%fused_computation.135 | convolution fusion | flops 4835770368 | bytes 18888704 | tf_op jit(solution)/shard_map/dot_general | solution.py:29
  453.1 14.8 %fusion.41 = f32[3072,768]{1,0:T(8,128)} fusion(bf16[1024,768]{0,1:T(8,128)(2,1)} %copy.138, f32[1024]{0:T(1024)S(1)} %copy-done.57, f32[1024,3072]{1,0:T(8,128)} %fusion.60, f32[3072]{0:T(1024)S(1)} %copy-done.59), kind=kOutput, calls=%fused_computation.76 | convolution fusion | flops 4865654784 | bytes 23609344 | tf_op jit(solution)/shard_map/dot_general | solution.py:29
  468.6 11.8 %add_convert_fusion.1 = bf16[1024,768]{0,1:T(8,128)(2,1)} fusion(f32[1024,768]{0,1:T(8,128)S(1)} %copy-done.3, bf16[3072,768]{1,0:T(8,128)(2,1)} %all-gather.12.cloned.1.call-done, f32[768]{0:T(1024)S(1)} %copy-done.63, f32[1024,3072]{1,0:T(8,128)} %fusion.60, f32[3072]{0:T(1024)S(1)} %copy-done.59), kind=kOutput, calls=%fused_computation.52 | convolution fusion | flops 4865654784 | bytes 22035456 | tf_op jit(solution)/shard_map/dot_general | solution.py:186
  480.4 2.6 copy.146
  483.1 9.0 fusion.77
  492.2 3.9 copy.143
  496.1 2.9 fusion.25
  499.1 40.5 %all-reduce.1 = f32[12,768]{1,0:T(8,128)S(1)} all-reduce(f32[12,768]{1,0:T(8,128)S(1)} %concatenate.34), channel_id=8, replica_groups=mesh['dp'=8,'blk'=4] {'dp','blk'}, use_global_device_ids=true, to_apply=%region_34.35.clone | all-reduce | flops 9216 | bytes 73728
  540.2 5.6 fusion.24
  547.4 83.4 %reduce-scatter.12.cloned.1.call-done = f32[24,2304]{1,0:T(8,128)} async-done(((f32[768,2304]{1,0:T(8,128)}), f32[24,2304]{1,0:T(8,128)}) %reduce-scatter.12.cloned.1.call-update) | async-done | bytes 221200 | tf_op jit(solution)/shard_map/reduce_scatter | solution.py:270
  633.7 137.6 %reduce-scatter.16.cloned.1.call-done = f32[24,3072]{1,0:T(8,128)} async-done(((f32[768,3072]{1,0:T(8,128)}), f32[24,3072]{1,0:T(8,128)}) %reduce-scatter.16.cloned.1.call-update) | async-done | bytes 294928 | tf_op jit(solution)/shard_map/reduce_scatter | solution.py:272
  773.6 139.4 %reduce-scatter.18.cloned.1.call-done = f32[96,768]{1,0:T(8,128)} async-done(((f32[3072,768]{1,0:T(8,128)}), f32[96,768]{1,0:T(8,128)}) %reduce-scatter.18.cloned.1.call-update) | async-done | bytes 294928 | tf_op jit(solution)/shard_map/reduce_scatter | solution.py:273
  916.1 3.7 copy.147
  919.8 39.8 %psum.7 = f32[]{:T(128)} all-reduce(f32[]{:T(128)S(6)} %add.250), channel_id=1, replica_groups=mesh['dp'=8,'blk'=4] {'dp','blk'}, use_global_device_ids=true, to_apply=%region_36.37 | all-reduce | flops 1 | bytes 8 | tf_op jit(solution)/shard_map/psum | solution.py:283
  (234 shorter events, 53.4 us)
Async XLA Ops:
  7.2 67.4 %all-gather.6.cloned.1.call-start = ((), (), s32[]{:S(2)}) async-start(), calls=%async_computation.6 | async-start | bytes 3649536 | tf_op jit(solution)/shard_map/all_gather | solution.py:137
  8.9 155.8 %all-gather.8.cloned.1.call-start = ((), (), s32[]{:S(2)}) async-start(), calls=%async_computation.7 | async-start | bytes 1216512 | tf_op jit(solution)/shard_map/all_gather | solution.py:138
  10.4 186.6 %all-gather.10.cloned.1.call-start = ((), (), s32[]{:S(2)}) async-start(), calls=%async_computation.8 | async-start | bytes 4866048 | tf_op jit(solution)/shard_map/all_gather | solution.py:139
  12.2 250.6 %all-gather.12.cloned.1.call-start = ((), (), s32[]{:S(2)}) async-start(), calls=%async_computation.9 | async-start | bytes 4866048 | tf_op jit(solution)/shard_map/all_gather | solution.py:140
  13.9 405.6 %reduce-scatter.22.cloned.1.call-start = ((), (), s32[]{:S(2)}) async-start(), calls=%async_computation.15 | async-start | bytes 983040
  59.4 15.2 %copy-start.47 = (f32[768]{0:T(1024)}, f32[768]{0:T(1024)S(1)}, u32[]{:S(2)}) copy-start(f32[768]{0:T(1024)S(1)} %get-tuple-element.151) | copy-start | bytes 9220
  59.4 15.2 %copy-start.64 = (f32[768]{0:T(1024)}, f32[768]{0:T(1024)S(1)}, u32[]{:S(2)}) copy-start(f32[768]{0:T(1024)S(1)} %get-tuple-element.150) | copy-start | bytes 9220
  65.2 15.7 %copy-start.45 = (f32[1024]{0:T(1024)}, f32[1024]{0:T(1024)S(1)}, u32[]{:S(2)}) copy-start(f32[1024]{0:T(1024)S(1)} %broadcast_multiply_fusion.5) | copy-start | bytes 12292
  65.7 15.3 %copy-start.49 = (f32[1024]{0:T(1024)}, f32[1024]{0:T(1024)S(1)}, u32[]{:S(2)}) copy-start(f32[1024]{0:T(1024)S(1)} %add_rsqrt_fusion.1) | copy-start | bytes 12292
  84.5 32.5 %copy-start.11 = (bf16[896,768]{0,1:T(8,128)(2,1)}, bf16[896,768]{0,1:T(8,128)(2,1)S(1)}, u32[]{:S(2)}) copy-start(bf16[896,768]{0,1:T(8,128)(2,1)S(1)} %copy.132) | copy-start | bytes 4128772
  132.7 15.2 %copy-start.29 = (f32[12,896]{1,0:T(8,128)}, f32[12,896]{1,0:T(8,128)S(1)}, u32[]{:S(2)}) copy-start(f32[12,896]{1,0:T(8,128)S(1)} %get-tuple-element.187) | copy-start | bytes 129028
  132.7 15.2 %copy-start.17 = (bf16[896,768]{0,1:T(8,128)(2,1)S(1)}, bf16[896,768]{0,1:T(8,128)(2,1)}, u32[]{:S(2)}) copy-start(bf16[896,768]{0,1:T(8,128)(2,1)} %copy.130) | copy-start | bytes 4128772
  147.9 16.7 %copy-start.66 = (f32[768]{0:T(1024)S(1)}, f32[768]{0:T(1024)}, u32[]{:S(2)}) copy-start(f32[768]{0:T(1024)} %get-tuple-element.147) | copy-start | bytes 9220
  147.9 16.7 %copy-start.69 = (bf16[12,64,128]{2,1,0:T(8,128)(2,1)S(1)}, bf16[12,64,128]{2,1,0:T(8,128)(2,1)}, u32[]{:S(2)}) copy-start(bf16[12,64,128]{2,1,0:T(8,128)(2,1)} %fusion.45) | copy-start | bytes 589828
  168.4 126.3 %copy-start.2 = (f32[1024,768]{0,1:T(8,128)}, f32[1024,768]{0,1:T(8,128)S(1)}, u32[]{:S(2)}) copy-start(f32[1024,768]{0,1:T(8,128)S(1)} %get-tuple-element.190) | copy-start | bytes 9437188
  168.4 28.6 %copy-start.31 = (f32[768]{0:T(1024)S(1)}, f32[768]{0:T(1024)}, u32[]{:S(2)}) copy-start(f32[768]{0:T(1024)} %get-tuple-element.144) | copy-start | bytes 9220
  168.5 28.5 %copy-start.32 = (f32[768]{0:T(1024)S(1)}, f32[768]{0:T(1024)}, u32[]{:S(2)}) copy-start(f32[768]{0:T(1024)} %get-tuple-element.146) | copy-start | bytes 9220
  197.0 65.8 %copy-start.57 = (f32[1024]{0:T(1024)S(1)}, f32[1024]{0:T(1024)}, u32[]{:S(2)}) copy-start(f32[1024]{0:T(1024)} %pad_convert_fusion) | copy-start | bytes 12292
  197.0 65.8 %copy-start.58 = (f32[3072]{0:T(1024)S(1)}, f32[3072]{0:T(1024)}, u32[]{:S(2)}) copy-start(f32[3072]{0:T(1024)} %add.232) | copy-start | bytes 36868
  262.8 17.4 %copy-start.19 = (bf16[768,3072]{1,0:T(8,128)(2,1)S(1)}, bf16[768,3072]{1,0:T(8,128)(2,1)}, u32[]{:S(2)}) copy-start(bf16[768,3072]{1,0:T(8,128)(2,1)} %all-gather.10.cloned.1.call-done) | copy-start | bytes 14155780
  316.3 29.9 %copy-start.1 = (f32[12,128,512]{2,1,0:T(8,128)S(1)}, f32[12,128,512]{2,1,0:T(8,128)}, u32[]{:S(2)}) copy-start(f32[12,128,512]{2,1,0:T(8,128)} %copy-done) | copy-start | bytes 9437188
  350.2 70.4 %reduce-scatter.20.cloned.1.call-start = ((), (), s32[]{:S(2)}) async-start(), calls=%async_computation.14 | async-start | bytes 983040
  364.8 181.1 %reduce-scatter.14.cloned.1.call-start = ((), (), s32[]{:S(2)}) async-start(), calls=%async_computation.11 | async-start | bytes 2433024 | tf_op jit(solution)/shard_map/reduce_scatter | solution.py:271
  364.8 31.5 %copy-start.10 = (bf16[896,768]{0,1:T(8,128)(2,1)S(1)}, bf16[896,768]{0,1:T(8,128)(2,1)}, u32[]{:S(2)}) copy-start(bf16[896,768]{0,1:T(8,128)(2,1)} %copy-done.9) | copy-start | bytes 4128772
  407.3 14.4 %copy-start.16 = (bf16[12,64,896]{2,1,0:T(8,128)(2,1)S(1)}, bf16[12,64,896]{2,1,0:T(8,128)(2,1)}, u32[]{:S(2)}) copy-start(bf16[12,64,896]{2,1,0:T(8,128)(2,1)} %fusion.30) | copy-start | bytes 4128772
  407.3 223.5 %reduce-scatter.12.cloned.1.call-start = ((), (), s32[]{:S(2)}) async-start(), calls=%async_computation.10 | async-start | bytes 7299072 | tf_op jit(solution)/shard_map/reduce_scatter | solution.py:270
  421.7 11.7 %copy-start.5 = (bf16[1024,768]{0,1:T(8,128)(2,1)S(1)}, bf16[1024,768]{0,1:T(8,128)(2,1)}, u32[]{:S(2)}) copy-start(bf16[1024,768]{0,1:T(8,128)(2,1)} %copy-done.4) | copy-start | bytes 4718596
  421.7 11.7 %copy-start.46 = (f32[1024]{0:T(1024)S(1)}, f32[1024]{0:T(1024)}, u32[]{:S(2)}) copy-start(f32[1024]{0:T(1024)} %copy-done.45) | copy-start | bytes 12292
  439.9 331.4 %reduce-scatter.16.cloned.1.call-start = ((), (), s32[]{:S(2)}) async-start(), calls=%async_computation.12 | async-start | bytes 9732096 | tf_op jit(solution)/shard_map/reduce_scatter | solution.py:272
  452.4 460.6 %reduce-scatter.18.cloned.1.call-start = ((), (), s32[]{:S(2)}) async-start(), calls=%async_computation.13 | async-start | bytes 9732096 | tf_op jit(solution)/shard_map/reduce_scatter | solution.py:273
  915.9 44.4 %copy-start.53 = (f32[12,24]{1,0:T(8,128)S(1)}, f32[12,24]{1,0:T(8,128)}, u32[]{:S(2)}) copy-start(f32[12,24]{1,0:T(8,128)} %param.27) | copy-start | bytes 3460
  915.9 44.4 %copy-start.61 = (f32[12,24]{1,0:T(8,128)S(1)}, f32[12,24]{1,0:T(8,128)}, u32[]{:S(2)}) copy-start(f32[12,24]{1,0:T(8,128)} %param.32) | copy-start | bytes 3460
  916.0 44.4 %copy-start.62 = (f32[12,24]{1,0:T(8,128)S(1)}, f32[12,24]{1,0:T(8,128)}, u32[]{:S(2)}) copy-start(f32[12,24]{1,0:T(8,128)} %param.37) | copy-start | bytes 3460
  916.0 45.1 %copy-start.38 = (f32[24,768]{1,0:T(8,128)S(1)}, f32[24,768]{1,0:T(8,128)}, u32[]{:S(2)}) copy-start(f32[24,768]{1,0:T(8,128)} %param.24) | copy-start | bytes 221188
  916.0 45.1 %copy-start.39 = (f32[24,768]{1,0:T(8,128)S(1)}, f32[24,768]{1,0:T(8,128)}, u32[]{:S(2)}) copy-start(f32[24,768]{1,0:T(8,128)} %reduce-scatter.14.cloned.1.call-done) | copy-start | bytes 221188
  916.0 45.1 %copy-start.44 = (f32[24,768]{1,0:T(8,128)S(1)}, f32[24,768]{1,0:T(8,128)}, u32[]{:S(2)}) copy-start(f32[24,768]{1,0:T(8,128)} %param.29) | copy-start | bytes 221188
  916.0 46.7 %copy-start.27 = (f32[24,2304]{1,0:T(8,128)S(1)}, f32[24,2304]{1,0:T(8,128)}, u32[]{:S(2)}) copy-start(f32[24,2304]{1,0:T(8,128)} %reduce-scatter.12.cloned.1.call-done) | copy-start | bytes 663556
  916.0 46.7 %copy-start.28 = (f32[24,2304]{1,0:T(8,128)S(1)}, f32[24,2304]{1,0:T(8,128)}, u32[]{:S(2)}) copy-start(f32[24,2304]{1,0:T(8,128)} %param.23) | copy-start | bytes 663556
  916.0 46.7 %copy-start.40 = (f32[24,2304]{1,0:T(8,128)S(1)}, f32[24,2304]{1,0:T(8,128)}, u32[]{:S(2)}) copy-start(f32[24,2304]{1,0:T(8,128)} %param.28) | copy-start | bytes 663556
  916.0 46.7 %copy-start.41 = (f32[24,2304]{1,0:T(8,128)S(1)}, f32[24,2304]{1,0:T(8,128)}, u32[]{:S(2)}) copy-start(f32[24,2304]{1,0:T(8,128)} %param.33) | copy-start | bytes 663556
  916.1 47.7 %copy-start.23 = (f32[96,768]{1,0:T(8,128)S(1)}, f32[96,768]{1,0:T(8,128)}, u32[]{:S(2)}) copy-start(f32[96,768]{1,0:T(8,128)} %param.26) | copy-start | bytes 884740
  916.1 47.7 %copy-start.26 = (f32[96,768]{1,0:T(8,128)S(1)}, f32[96,768]{1,0:T(8,128)}, u32[]{:S(2)}) copy-start(f32[96,768]{1,0:T(8,128)} %reduce-scatter.18.cloned.1.call-done) | copy-start | bytes 884740
  916.1 47.7 %copy-start.34 = (f32[96,768]{1,0:T(8,128)S(1)}, f32[96,768]{1,0:T(8,128)}, u32[]{:S(2)}) copy-start(f32[96,768]{1,0:T(8,128)} %param.31) | copy-start | bytes 884740
  916.1 47.7 %copy-start.35 = (f32[96,768]{1,0:T(8,128)S(1)}, f32[96,768]{1,0:T(8,128)}, u32[]{:S(2)}) copy-start(f32[96,768]{1,0:T(8,128)} %param.36) | copy-start | bytes 884740
  919.8 45.0 %copy-start.24 = (f32[24,3072]{1,0:T(8,128)S(1)}, f32[24,3072]{1,0:T(8,128)}, u32[]{:S(2)}) copy-start(f32[24,3072]{1,0:T(8,128)} %param.25) | copy-start | bytes 884740
  919.8 45.0 %copy-start.25 = (f32[24,3072]{1,0:T(8,128)S(1)}, f32[24,3072]{1,0:T(8,128)}, u32[]{:S(2)}) copy-start(f32[24,3072]{1,0:T(8,128)} %reduce-scatter.16.cloned.1.call-done) | copy-start | bytes 884740
  919.8 45.0 %copy-start.36 = (f32[24,3072]{1,0:T(8,128)S(1)}, f32[24,3072]{1,0:T(8,128)}, u32[]{:S(2)}) copy-start(f32[24,3072]{1,0:T(8,128)} %param.30) | copy-start | bytes 884740
  919.8 45.0 %copy-start.37 = (f32[24,3072]{1,0:T(8,128)S(1)}, f32[24,3072]{1,0:T(8,128)}, u32[]{:S(2)}) copy-start(f32[24,3072]{1,0:T(8,128)} %param.35) | copy-start | bytes 884740
  (33 other events, 120.7 us)
Sparse Core Ops, SparseCore 0:
  11.5 62.9 all-gather.5
  78.0 52.9 all-gather.7
  134.5 62.4 all-gather.9
  200.3 62.3 all-gather.11
  350.3 22.0 reduce-scatter.21
  375.0 23.2 reduce-scatter.19
  407.4 98.5 reduce-scatter.13
  512.6 118.1 reduce-scatter.11
  636.7 134.5 reduce-scatter.15
  778.0 134.8 reduce-scatter.17
where the time goes:
time: 981 us; the launch traced here: 974 us
  waiting for transfers between devices  449 us (46%)
  matrix products  216 us (22%)
  blocking collectives  142 us (14%)
  other arithmetic  95.7 us (10%)
  local copies, waits for them, and re-layouts  50 us (5%)
  between operations  21 us (2%)
    reduce_scatter x1, waiting for transfers between devices, per_device(): lax.psum_scatter(grad_down, ('dp', 'blk'), scatter_dimension=0, tiled=True)  139 us
    reduce_scatter x1, waiting for transfers between devices, per_device(): lax.psum_scatter(grad_up, ('dp', 'blk'), scatter_dimension=0, tiled=True)  138 us
    reduce_scatter x1, waiting for transfers between devices, per_device(): lax.psum_scatter(grad_qkv, ('dp', 'blk'), scatter_dimension=0, tiled=True)  83.4 us
    all_gather x1, waiting for transfers between devices, per_device(): lax.all_gather(low_down, ('dp', 'blk'), axis=0, tiled=True)  54.7 us
    all_gather x1, blocking collectives, per_device(): lax.all_gather(low_vec, ('dp', 'blk'), axis=1, tiled=True)  43.7 us
    unnamed x1, blocking collectives  40.5 us
    psum x1, blocking collectives, per_device(): square_sum = lax.psum(local_square, ('dp', 'blk'))  39.8 us
    dot_general x4, matrix products, outer_sum(): lax.dot_general(left_side, right_side, (((0,), (0,)), ((), ())), preferre...  36.1 us
  transfers between devices with their start and end apart: 10, of which 6 were waited for; matrix products, arithmetic and copies ran while one was open for 26% of the time, Pallas kernels for 0%

commit v1 on v0

v1 whole, which is shorter than its diff:
```python
import functools

import jax
import jax.numpy as jnp
from jax import lax
from jax.experimental import pallas as pl
from jax.experimental.pallas import tpu as pltpu
from jax.sharding import PartitionSpec as P

HD = 64
SHORT_DEV = 896
LONG_DEV = 128
STEP = 10
TILE = 128
BAND = 3 * TILE
PAIR = 2 * HD
ROWS = 256

eps_norm = 1e-06
far_below = -1000000000.0
rate_matrix = 0.04
rate_vector = 0.5
beta_first = 0.5
beta_second = 0.5
eps_adam = 1e-08
decay_weight = 0.01
score_scale = HD ** (-0.5)
gelu_root = 0.7978845608028654
gelu_cube = 0.044715
VMEM_MOST = 60 * 1024 * 1024
FUSED_VMEM = 63 * 1024 * 1024


def dot(left, right):
    return lax.dot_general(left, right, (((1,), (0,)), ((), ())), preferred_element_type=jnp.float32)


def dot_tr(left, right):
    return lax.dot_general(left, right, (((1,), (1,)), ((), ())), preferred_element_type=jnp.float32)


def dot_tl(left, right):
    return lax.dot_general(left, right, (((0,), (0,)), ((), ())), preferred_element_type=jnp.float32)


def standardize(values):
    centered = values - jnp.mean(values, -1, keepdims=True)
    inv_std = lax.rsqrt(jnp.mean(centered * centered, -1, keepdims=True) + eps_norm)
    return centered * inv_std, inv_std


def norm_back(upstream, standard, inv_std, gain):
    scaled = upstream * gain
    inner = (
        scaled
        - jnp.mean(scaled, -1, keepdims=True)
        - standard * jnp.mean(scaled * standard, -1, keepdims=True)
    )
    return inner * inv_std


def column_sum(values):
    return jnp.sum(values, 0, keepdims=True)


def rows_at(step):
    return pl.ds(pl.multiple_of(step * ROWS, ROWS), ROWS)


def qkv_phase(x_ref, vec_ref, w_ref, h1_ref, qkv_ref):
    width = x_ref.shape[1]

    @pl.loop(0, x_ref.shape[0] // ROWS)
    def _(step):
        here = rows_at(step)
        unit, _ = standardize(x_ref[here, :].astype(jnp.float32))
        hidden = (unit * vec_ref[0:1, :] + vec_ref[1:2, :]).astype(jnp.bfloat16)
        h1_ref[here, :] = hidden
        for part, bias in ((0, 4), (1, None), (2, 5)):
            columns = slice(part * width, (part + 1) * width)
            made = dot(hidden, w_ref[:, columns])
            if bias is not None:
                made = made + vec_ref[bias : bias + 1, :]
            qkv_ref[here, columns] = made.astype(jnp.bfloat16)


def stack_heads(values, scale):
    lane = lax.broadcasted_iota(jnp.int32, values.shape, 1)
    if scale is not None:
        values = values * jnp.asarray(scale, values.dtype)
    zero = jnp.zeros_like(values)
    return jnp.concatenate(
        [jnp.where(lane < HD, values, zero), jnp.where(lane < HD, zero, values)], 0
    )


def unstack_heads(values):
    return jnp.concatenate([values[:HD, :TILE], values[HD:, TILE:]], 0)


def softmax_of(scores, allowed):
    scores = jnp.where(allowed, scores, far_below)
    top = jnp.max(scores, 0, keepdims=True)
    exponent = jnp.exp(scores - top)
    total = jnp.sum(exponent, 0, keepdims=True)
    return (exponent * (1.0 / total)).astype(jnp.bfloat16), top + jnp.log(total)


def attend_forward(queries, keys, values_tr, allowed):
    probs, log_total = softmax_of(dot_tr(keys, stack_heads(queries, score_scale)), allowed)
    return unstack_heads(dot(values_tr, probs)).astype(jnp.bfloat16), log_total


def softmax_back(scores, allowed, log_total, grad_probs):
    probs = jnp.exp(jnp.where(allowed, scores, far_below) - log_total)
    delta = jnp.sum(probs * grad_probs, 0, keepdims=True)
    grad_scores = (probs * (grad_probs - delta)).astype(jnp.bfloat16)
    return probs.astype(jnp.bfloat16), grad_scores


def attend_back(queries, keys, keys_tr, values, allowed, log_total, upstream):
    stacked_q = stack_heads(queries, score_scale)
    stacked_up = stack_heads(upstream, None)
    probs, grad_scores = softmax_back(
        dot_tr(keys, stacked_q), allowed, log_total, dot_tr(values, stacked_up)
    )
    grad_keys = dot(grad_scores, stacked_q)
    grad_values = dot(probs, stacked_up)
    grad_queries = unstack_heads(dot(keys_tr, grad_scores)) * score_scale
    return grad_queries.astype(jnp.bfloat16).T, grad_keys, grad_values


def mark_segments(ends_ref, key_seg, query_seg):
    count = ends_ref.shape[1]
    for tile in range(SHORT_DEV // TILE):
        rows = lax.broadcasted_iota(jnp.int32, (TILE, TILE), 0) + tile * TILE
        lanes = lax.broadcasted_iota(jnp.int32, (1, TILE), 1) + tile * TILE
        by_row = jnp.zeros((TILE, TILE), jnp.float32)
        by_lane = jnp.zeros((1, TILE), jnp.float32)
        end = jnp.int32(0)
        for clip in range(count):
            end = end + ends_ref[0, clip]
            by_row = by_row + jnp.where(rows >= end, 1.0, 0.0)
            by_lane = by_lane + jnp.where(lanes >= end, 1.0, 0.0)
        key_seg[tile * TILE : (tile + 1) * TILE, :] = by_row
        query_seg[tile] = by_lane


def band_start(tile):
    most = SHORT_DEV - BAND
    return pl.multiple_of(jnp.clip((tile - 1) * TILE, 0, most), TILE)


def pair_lanes(pair, offset=0):
    return pl.ds(pl.multiple_of(offset + pair * PAIR, PAIR), PAIR)


def short_mask(tile, key_seg, query_seg):
    band = key_seg[pl.ds(band_start(tile), BAND), :]
    line = query_seg[tile]
    return jnp.concatenate([band, band], 1) == jnp.concatenate([line, line], 1)


def long_mask(length_ref, keys):
    place = lax.broadcasted_iota(jnp.int32, (keys, 2 * TILE), 0)
    return place < length_ref[0]


def attention_forward_phase(qkv_ref, far_ref, length_ref, key_seg, query_seg, out_ref, lse_ref):
    width = out_ref.shape[1]
    pairs = width // PAIR
    tiles = SHORT_DEV // TILE

    @pl.loop(0, tiles)
    def _(tile):
        rows = pl.ds(pl.multiple_of(tile * TILE, TILE), TILE)
        band = pl.ds(band_start(tile), BAND)
        allowed = short_mask(tile, key_seg, query_seg)
        for pair in range(pairs):
            made, lse = attend_forward(
                qkv_ref[rows, pair * PAIR : (pair + 1) * PAIR],
                qkv_ref[band, width + pair * PAIR : width + (pair + 1) * PAIR],
                qkv_ref[band, 2 * width + pair * PAIR : 2 * width + (pair + 1) * PAIR].T,
                allowed,
            )
            out_ref[rows, pair * PAIR : (pair + 1) * PAIR] = made.T
            lse_ref[tile, pair] = lse

    @pl.loop(0, pairs)
    def _(pair):
        allowed = long_mask(length_ref, far_ref.shape[0])
        made, lse = attend_forward(
            qkv_ref[SHORT_DEV:, pair_lanes(pair)],
            far_ref[:, pair_lanes(pair)],
            far_ref[:, pair_lanes(pair, width)].T,
            allowed,
        )
        out_ref[SHORT_DEV:, pair_lanes(pair)] = made.T
        lse_ref[tiles, pair] = lse


def attention_back_long(qkv_ref, far_ref, length_ref, lse_ref, up_ref, dqkv_ref, far_grad):
    width = up_ref.shape[1]
    tiles = SHORT_DEV // TILE

    @pl.loop(0, width // PAIR)
    def _(pair):
        allowed = long_mask(length_ref, far_ref.shape[0])
        dq, dk, dv = attend_back(
            qkv_ref[SHORT_DEV:, pair_lanes(pair)],
            far_ref[:, pair_lanes(pair)],
            far_ref[:, pair_lanes(pair)].T,
            far_ref[:, pair_lanes(pair, width)],
            allowed,
            lse_ref[tiles, pair],
            up_ref[SHORT_DEV:, pair_lanes(pair)],
        )
        dqkv_ref[SHORT_DEV:, pair_lanes(pair)] = dq
        far_grad[:, pair_lanes(pair)] = dk.astype(jnp.bfloat16)
        far_grad[:, pair_lanes(pair, width)] = dv.astype(jnp.bfloat16)


def attention_back_short(qkv_ref, key_seg, query_seg, lse_ref, up_ref, dqkv_ref, dk_acc, dv_acc):
    width = up_ref.shape[1]
    tiles = SHORT_DEV // TILE

    @pl.loop(0, width // (2 * PAIR))
    def _(group):
        dk_acc[...] = jnp.zeros_like(dk_acc)
        dv_acc[...] = jnp.zeros_like(dv_acc)

        @pl.loop(0, tiles)
        def _(tile):
            rows = pl.ds(pl.multiple_of(tile * TILE, TILE), TILE)
            band = pl.ds(band_start(tile), BAND)
            allowed = short_mask(tile, key_seg, query_seg)
            for half in range(2):
                pair = group * 2 + half
                dq, dk, dv = attend_back(
                    qkv_ref[rows, pair_lanes(pair)],
                    qkv_ref[band, pair_lanes(pair, width)],
                    qkv_ref[band, pair_lanes(pair, width)].T,
                    qkv_ref[band, pair_lanes(pair, 2 * width)],
                    allowed,
                    lse_ref[tile, pair],
                    up_ref[rows, pair_lanes(pair)],
                )
                dqkv_ref[rows, pair_lanes(pair)] = dq
                own = slice(half * PAIR, (half + 1) * PAIR)
                dk_acc[band, own] += dk
                dv_acc[band, own] += dv

        lanes = 2 * PAIR
        k_at = pl.ds(pl.multiple_of(width + group * lanes, lanes), lanes)
        v_at = pl.ds(pl.multiple_of(2 * width + group * lanes, lanes), lanes)
        dqkv_ref[:SHORT_DEV, k_at] = dk_acc[...].astype(jnp.bfloat16)
        dqkv_ref[:SHORT_DEV, v_at] = dv_acc[...].astype(jnp.bfloat16)


def middle_phase(x_ref, vec_ref, w_ref, att_ref, middle_ref, h2_ref):
    @pl.loop(0, x_ref.shape[0] // ROWS)
    def _(step):
        here = rows_at(step)
        made = dot(att_ref[here, :], w_ref[...]) + vec_ref[6:7, :]
        middle = x_ref[here, :].astype(jnp.float32) + made
        middle_ref[here, :] = middle
        unit, _ = standardize(middle)
        h2_ref[here, :] = (unit * vec_ref[2:3, :] + vec_ref[3:4, :]).astype(jnp.bfloat16)


def gelu_both(values):
    square = values * values
    inner = values * (gelu_root + (gelu_root * gelu_cube) * square)
    bent = jnp.tanh(inner)
    half_up = 0.5 + 0.5 * bent
    slope = half_up + (0.5 * values) * (1.0 - bent * bent) * (
        gelu_root + (3.0 * gelu_root * gelu_cube) * square
    )
    return values * half_up, slope


def mlp_rows(h2_ref, dy_ref, up_ref, down_ref, bias, act_ref, du_ref, out_acc, dh2_acc, first):
    def body(step, total):
        here = rows_at(step)
        pre = dot(h2_ref[here, :], up_ref[...]) + bias
        grad_act = dot_tr(dy_ref[here, :], down_ref[...])
        act, slope = gelu_both(pre)
        act_low = act.astype(jnp.bfloat16)
        du_low = (grad_act * slope).astype(jnp.bfloat16)
        act_ref[here, :] = act_low
        du_ref[here, :] = du_low
        made = dot(act_low, down_ref[...])
        grad_hidden = dot_tr(du_low, up_ref[...])
        if first is True:
            out_acc[here, :] = made
            dh2_acc[here, :] = grad_hidden
        else:
            out_acc[here, :] += made
            dh2_acc[here, :] += grad_hidden
        return total + column_sum(du_low.astype(jnp.float32))

    width = up_ref.shape[1]
    return lax.fori_loop(0, h2_ref.shape[0] // ROWS, body, jnp.zeros((1, width), jnp.float32))


def middle_back_phase(
    dy_ref, middle_ref, dh2_ref, vec_ref, w_ref, dmiddle_ref, da_ref, datt_ref, gvec_ref
):
    def body(step, totals):
        here = rows_at(step)
        dy_low = dy_ref[here, :].astype(jnp.float32)
        dh2 = dh2_ref[here, :]
        unit, inv_std = standardize(middle_ref[here, :])
        dmiddle = dy_low + norm_back(dh2, unit, inv_std, vec_ref[2:3, :])
        dmiddle_ref[here, :] = dmiddle
        da = dmiddle.astype(jnp.bfloat16)
        da_ref[here, :] = da
        datt_ref[here, :] = dot_tr(da, w_ref[...]).astype(jnp.bfloat16)
        return (
            totals[0] + column_sum(dh2 * unit),
            totals[1] + column_sum(dh2),
            totals[2] + column_sum(da.astype(jnp.float32)),
            totals[3] + column_sum(dy_low),
        )

    zero = jnp.zeros((1, dy_ref.shape[1]), jnp.float32)
    totals = lax.fori_loop(0, dy_ref.shape[0] // ROWS, body, (zero,) * 4)
    for place in range(4):
        gvec_ref[place : place + 1, :] = totals[place]


def input_back_phase(x_ref, dqkv_ref, vec_ref, w_ref, dmiddle_ref, grad_ref, gvec_ref):
    width = x_ref.shape[1]

    def body(step, totals):
        here = rows_at(step)
        dh1 = dot_tr(dqkv_ref[here, :], w_ref[...])
        unit, inv_std = standardize(x_ref[here, :].astype(jnp.float32))
        grad_ref[here, :] = dmiddle_ref[here, :] + norm_back(dh1, unit, inv_std, vec_ref[0:1, :])
        return (
            totals[0] + column_sum(dh1 * unit),
            totals[1] + column_sum(dh1),
            totals[2] + column_sum(dqkv_ref[here, :width].astype(jnp.float32)),
            totals[3] + column_sum(dqkv_ref[here, 2 * width :].astype(jnp.float32)),
        )

    zero = jnp.zeros((1, width), jnp.float32)
    totals = lax.fori_loop(0, x_ref.shape[0] // ROWS, body, (zero,) * 4)
    for place in range(4):
        gvec_ref[place : place + 1, :] = totals[place]


def call(body, outs, scratch=(), smem=()):
    def run(*arrays):
        specs = [
            pl.BlockSpec(memory_space=pltpu.SMEM if place in smem else pltpu.VMEM)
            for place in range(len(arrays))
        ]
        return pl.pallas_call(
            body,
            out_shape=[jax.ShapeDtypeStruct(shape, kind) for shape, kind in outs],
            in_specs=specs,
            out_specs=[pl.BlockSpec(memory_space=pltpu.VMEM)] * len(outs),
            scratch_shapes=list(scratch),
            compiler_params=pltpu.CompilerParams(vmem_limit_bytes=VMEM_MOST),
        )(*arrays)

    return run


def forward_kernel(
    ends_ref, length_ref, x_ref, vec_ref, qkv_ref, far_ref, w_ref,
    att_ref, lse_ref, middle_ref, h2_ref, key_seg, query_seg,
):
    mark_segments(ends_ref, key_seg, query_seg)
    attention_forward_phase(qkv_ref, far_ref, length_ref, key_seg, query_seg, att_ref, lse_ref)
    middle_phase(x_ref, vec_ref, w_ref, att_ref, middle_ref, h2_ref)


def mlp_kernel(
    h2_ref, dy_ref, middle_ref, up_ref, down_ref, bias_ref, last_ref,
    out_ref, dh2_ref, gup_ref, gdown_ref, gbu_ref, act_ref, du_ref, out_acc,
):
    block = pl.program_id(0)

    @pl.when(block == 0)
    def _():
        out_acc[...] = jnp.zeros_like(out_acc)
        dh2_ref[...] = jnp.zeros_like(dh2_ref)

    gbu_ref[0] = mlp_rows(
        h2_ref, dy_ref, up_ref, down_ref, bias_ref[0], act_ref, du_ref, out_acc, dh2_ref, None
    )
    gup_ref[...] = dot_tl(h2_ref[...], du_ref[...])
    gdown_ref[...] = dot_tl(act_ref[...], dy_ref[...])

    @pl.when(block == pl.num_programs(0) - 1)
    def _():
        out_ref[...] = (middle_ref[...] + (out_acc[...] + last_ref[...])).astype(jnp.bfloat16)


def run_mlp(h2, dy, middle, w_up, w_down, bias_up, bias_down):
    rows, width = h2.shape
    units = w_up.shape[1]
    blocks = units // width
    whole = lambda shape: pl.BlockSpec(shape, lambda b: (0, 0))
    return pl.pallas_call(
        mlp_kernel,
        grid=(blocks,),
        out_shape=[
            jax.ShapeDtypeStruct((rows, width), jnp.bfloat16),
            jax.ShapeDtypeStruct((rows, width), jnp.float32),
            jax.ShapeDtypeStruct((width, units), jnp.float32),
            jax.ShapeDtypeStruct((units, width), jnp.float32),
            jax.ShapeDtypeStruct((blocks, 1, width), jnp.float32),
        ],
        in_specs=[
            whole((rows, width)),
            whole((rows, width)),
            whole((rows, width)),
            pl.BlockSpec((width, width), lambda b: (0, b)),
            pl.BlockSpec((width, width), lambda b: (b, 0)),
            pl.BlockSpec((1, 1, width), lambda b: (b, 0, 0)),
            whole((1, width)),
        ],
        out_specs=[
            whole((rows, width)),
            whole((rows, width)),
            pl.BlockSpec((width, width), lambda b: (0, b)),
            pl.BlockSpec((width, width), lambda b: (b, 0)),
            pl.BlockSpec((1, 1, width), lambda b: (b, 0, 0)),
        ],
        scratch_shapes=[
            pltpu.VMEM((rows, width), jnp.bfloat16),
            pltpu.VMEM((rows, width), jnp.bfloat16),
            pltpu.VMEM((rows, width), jnp.float32),
        ],
        compiler_params=pltpu.CompilerParams(vmem_limit_bytes=VMEM_MOST),
    )(h2, dy, middle, w_up, w_down, bias_up, bias_down)


def middle_back_kernel(
    dy_ref, middle_ref, dh2_ref, vec_ref, w_ref, att_ref,
    dmiddle_ref, datt_ref, gvec_ref, gout_ref, da_ref,
):
    middle_back_phase(
        dy_ref, middle_ref, dh2_ref, vec_ref, w_ref, dmiddle_ref, da_ref, datt_ref, gvec_ref
    )
    gout_ref[...] = dot_tl(att_ref[...], da_ref[...])


def attention_back_kernel(
    ends_ref, length_ref, qkv_ref, far_ref, lse_ref, datt_ref,
    dqkv_ref, far_grad, key_seg, query_seg, dk_acc, dv_acc,
):
    mark_segments(ends_ref, key_seg, query_seg)
    attention_back_long(qkv_ref, far_ref, length_ref, lse_ref, datt_ref, dqkv_ref, far_grad)
    width = datt_ref.shape[1]
    dqkv_ref[SHORT_DEV:, width:] = jnp.zeros((LONG_DEV, 2 * width), jnp.bfloat16)
    attention_back_short(
        qkv_ref, key_seg, query_seg, lse_ref, datt_ref, dqkv_ref, dk_acc, dv_acc
    )


def input_back_kernel(
    x_ref, h1_ref, dqkv_ref, near_ref, vec_ref, w_ref, dmiddle_ref,
    grad_ref, gqkv_ref, gvec_ref, mixed_ref,
):
    width = x_ref.shape[1]
    mixed_ref[...] = dqkv_ref[...]
    mixed_ref[SHORT_DEV:, width:] = near_ref[...]
    input_back_phase(x_ref, mixed_ref, vec_ref, w_ref, dmiddle_ref, grad_ref, gvec_ref)
    for part in range(3):
        columns = slice(part * width, (part + 1) * width)
        gqkv_ref[:, columns] = dot_tl(h1_ref[...], mixed_ref[:, columns])


def when(condition, body):
    if isinstance(condition, bool):
        if condition:
            body()
    else:
        pl.when(condition)(body)


def both(left, right):
    if isinstance(left, bool) and isinstance(right, bool):
        return left and right
    return jnp.logical_and(left, right)


class Places:
    def __init__(self, depth):
        self.depth = depth
        dp, blk = lax.axis_index("dp"), lax.axis_index("blk")
        self.dp, self.blk = dp, blk
        z, x, y, c = dp // 2, lax.rem(dp, 2), blk // 2, lax.rem(blk, 2)
        self.z, self.x, self.y, self.c = z, x, y, c
        flip = lambda value, by: lax.rem(value + by, 2)
        self.core = (dp, y * 2 + 1 - c)
        self.x_peer = (z * 2 + 1 - x, blk)
        self.y_peer = (dp, (1 - y) * 2 + c)
        self.first = (z * 2 + flip(x, 1 - c), flip(y, c) * 2 + c)
        self.second = (z * 2 + flip(x, c), flip(y, 1 - c) * 2 + c)
        self.corner = x * 4 + blk
        self.s, self.f = jnp.where(c == 0, y, x), jnp.where(c == 0, x, y)
        self.own = self.s * 2 + self.f
        self.at_first = self.s * 2 + 1 - self.f
        self.near_two = pl.ds(2 * self.s, 2)
        self.far_two = pl.ds(2 - 2 * self.s, 2)
        self.core_near_two = pl.ds(2 * self.f, 2)
        self.core_far_two = pl.ds(2 - 2 * self.f, 2)

    def z_peer(self, step):
        return (lax.rem(self.z + step, self.depth) * 2 + self.x, self.blk)

    def z_from(self, step):
        return lax.rem(self.z - step + self.depth, self.depth)

    def z_to(self, step):
        return lax.rem(self.z + step, self.depth)

    def plane_from(self, step):
        return lax.rem(self.corner - step + 8, 8)

    def plane_peer(self, step):
        corner = lax.rem(self.corner + step, 8)
        return (self.z * 2 + corner // 4, lax.rem(corner, 4))


def remote(source, target, sends, recvs, device):
    return pltpu.make_async_remote_copy(
        src_ref=source,
        dst_ref=target,
        send_sem=sends,
        recv_sem=recvs,
        device_id=device,
        device_id_type=pl.DeviceIdType.MESH,
    )


class Gather:
    def __init__(self, at, pieces, sends, recvs, plane=None):
        self.at, self.pieces, self.sends, self.recvs, self.plane = at, pieces, sends, recvs, plane
        self.near = at.depth - 1

    def along_z(self, block, step, whole, incoming):
        at = self.at
        source = at.z_from(step) if incoming else at.z
        region = self.pieces(block, None if whole else source, at.own, True)
        index = step - 1
        return remote(
            region, region, self.sends.at[block, index], self.recvs.at[block, index],
            at.z_peer(step),
        )

    def copy(self, block, kind, incoming=False):
        at = self.at
        device = (at.first, at.second, at.core, at.core)[kind]
        going = (at.own, at.near_two, at.near_two, at.far_two)
        coming = (at.at_first, at.far_two, at.core_near_two, at.core_far_two)
        place = (coming if incoming else going)[kind]
        region = self.pieces(block, None, place, not (incoming and kind >= 2))
        index = self.near + kind
        return remote(
            region, region, self.sends.at[block, index], self.recvs.at[block, index], device
        )

    def start(self, block, *kinds):
        for kind in kinds:
            self.copy(block, kind).start()

    def arrive(self, block, *kinds):
        for kind in kinds:
            self.copy(block, kind, True).wait_recv()

    def split(self, block, every, one):
        if self.plane is None:
            every()
            return
        single, z = self.plane(block)
        if isinstance(single, bool):
            one(z) if single else every()
            return
        pl.when(single)(lambda: one(z))
        pl.when(jnp.logical_not(single))(every)

    def push(self, block):
        def every():
            for step in range(1, self.at.depth):
                self.along_z(block, step, False, False).start()

        def one(z):
            @pl.when(self.at.z == z)
            def _():
                for step in range(1, self.at.depth):
                    self.along_z(block, step, True, False).start()

        self.split(block, every, one)

    def stage_two(self, block):
        def every():
            for step in range(1, self.at.depth):
                self.along_z(block, step, False, True).wait_recv()

        def one(z):
            @pl.when(self.at.z != z)
            def _():
                away = lax.rem(self.at.z - z + self.at.depth, self.at.depth)
                self.along_z(block, away, True, True).wait_recv()

        self.split(block, every, one)
        self.start(block, 0)

    def stage_three(self, block):
        self.arrive(block, 0)
        self.start(block, 1, 2)

    def stage_four(self, block):
        self.arrive(block, 1)
        self.start(block, 3)

    def finish(self, block):
        self.arrive(block, 2, 3)

    def sent(self, block):
        def every():
            for step in range(1, self.at.depth):
                self.along_z(block, step, False, False).wait_send()

        def one(z):
            @pl.when(self.at.z == z)
            def _():
                for step in range(1, self.at.depth):
                    self.along_z(block, step, True, False).wait_send()

        self.split(block, every, one)
        for kind in range(4):
            self.copy(block, kind).wait_send()


class Exchange:
    def __init__(self, at, sent, got, got_z, sends, recvs, slot):
        self.at, self.sent, self.got, self.got_z = at, sent, got, got_z
        self.sends, self.recvs, self.slot = sends, recvs, slot
        self.stage, self.copies, self.value = 0, [], None

    def copy(self, source, target, index, device):
        return remote(
            source, target, self.sends.at[self.slot, index], self.recvs.at[self.slot, index], device
        )

    def begin(self, value):
        at, stage = self.at, self.stage
        self.value = value
        self.sent[stage] = value
        peers = (at.core, at.x_peer, at.y_peer)
        if stage < 3:
            copy = self.copy(self.sent.at[stage], self.got.at[stage], stage, peers[stage])
            self.copies = [(copy, copy)]
        else:
            self.got_z[at.z] = value
            self.copies = []
            for step in range(1, at.depth):
                ends = [self.got_z.at[at.z], self.got_z.at[at.z_from(step)]]
                self.copies.append(
                    tuple(self.copy(self.sent.at[3], end, 2 + step, at.z_peer(step)) for end in ends)
                )
        for going, _ in self.copies:
            going.start()

    def step(self):
        for going, coming in self.copies:
            going.wait_send()
            coming.wait_recv()
        if self.stage < 3:
            value = self.value + self.got[self.stage]
            self.stage += 1
            self.begin(value)
            return None
        value = self.got_z[0]
        for place in range(1, self.at.depth):
            value = value + self.got_z[place]
        return value


class ShortExchange:
    def __init__(self, at, sent, got_z, got_plane, sends, recvs):
        self.at, self.sent, self.got_z, self.got_plane = at, sent, got_z, got_plane
        self.sends, self.recvs = sends, recvs

    def start(self, stage, landing, mine, value, others):
        self.sent[stage] = value
        landing[mine] = value
        copies = []
        for device, slot, index in others:
            ends = [landing.at[mine], landing.at[slot]]
            copies.append(
                tuple(
                    remote(self.sent.at[stage], end, self.sends.at[index], self.recvs.at[index], device)
                    for end in ends
                )
            )
        for going, _ in copies:
            going.start()
        return copies

    def finish(self, landing, copies):
        for going, coming in copies:
            going.wait_send()
            coming.wait_recv()
        value = landing[0]
        for place in range(1, landing.shape[0]):
            value = value + landing[place]
        return value

    def along_z(self, value):
        at = self.at
        others = [(at.z_peer(step), at.z_from(step), step - 1) for step in range(1, at.depth)]
        return self.start(0, self.got_z, at.z, value, others)

    def in_plane(self, value):
        at = self.at
        others = [
            (at.plane_peer(step), at.plane_from(step), at.depth - 2 + step) for step in range(1, 8)
        ]
        return self.start(1, self.got_plane, at.corner, value, others)


def fused_kernel(
    depth, ends_ref, length_ref, wqkv_ref, wout_ref, wup_ref, wdown_ref, vectors_ref, x_hbm, cot_hbm,
    out_hbm, grad_hbm, rqkv_ref, rout_ref, rup_ref, rdown_ref, rvec_ref, norm_ref,
    w, vbuf, vpad, give_out, asm, asm_down, vec, qkv, att, middle, h2, act, du, out_acc, dh2, dy,
    far, far_got, lse, key_seg, query_seg, turned, h2_tr, flat_up, flat_down,
    got_a, got_b, got_z, got_zd, red, squares, gvec,
    v_sent, v_got, v_got_z, n_sent, n_got, n_got_z,
    swap_s, swap_r, ag_s, ag_r, vg_s, vg_r, kv_s, kv_r, fg_s, fg_r, rs_s, rs_r, ex_s, ex_r, no_s, no_r, local_s,
):
    bf16, f32 = jnp.bfloat16, jnp.float32
    at = Places(depth)
    rows, width = dy.shape
    spare = w.shape[0] - 2
    blocks = spare
    slab = w.shape[4]
    share = slab // 2
    half = width // 2
    lanes4 = 2 * PAIR
    groups = width // lanes4
    units = (blocks - groups - 1) // 2
    tiles = SHORT_DEV // TILE
    mine = pl.ds(pl.multiple_of(at.c * half, 128), half)
    other = pl.ds(pl.multiple_of((1 - at.c) * half, 128), half)
    my_rows = pl.ds(pl.multiple_of(at.c * share, 8), share)
    other_rows = pl.ds(pl.multiple_of((1 - at.c) * share, 8), share)
    tall = units * share
    my_tall = pl.ds(pl.multiple_of(at.c * tall, 8), tall)
    other_tall = pl.ds(pl.multiple_of((1 - at.c) * tall, 8), tall)
    wide = 2 * PAIR
    wide_at = lambda step: pl.ds(pl.multiple_of(step * wide, wide), wide)

    barrier = pltpu.get_barrier_semaphore()
    friends = [at.plane_peer(step) for step in range(1, 8)]
    friends += [at.z_peer(step) for step in range(1, depth)]
    for friend in friends:
        pl.semaphore_signal(barrier, inc=1, device_id=friend, device_id_type=pl.DeviceIdType.MESH)
    load_x = pltpu.make_async_copy(x_hbm, dy, local_s.at[0])
    load_x.start()

    def pair_part(part, pair):
        return pl.ds(pl.multiple_of(part * width + pair * PAIR, PAIR), PAIR)

    def own_slot(slot, side, columns):
        if slot < groups:
            parts = [lax.rem(place + side, 3) for place in range(3)]
            return [wqkv_ref[:, pair_part(part, 2 * slot + side)] for part in parts]
        if slot == groups:
            return [wout_ref[:, columns]]
        start = (slot - groups - 1) * width
        return [wup_ref[:, pl.ds(pl.multiple_of(start + side * half, 128), half)]]

    slots = groups + 1 + units
    for slot in range(slots):
        lane = 0
        for piece in own_slot(slot, 1 - at.c, other):
            give_out[slot, :, lane : lane + piece.shape[1]] = piece
            lane += piece.shape[1]
    vpad[...] = jnp.zeros_like(vpad)
    vpad[: vectors_ref.shape[0], : vectors_ref.shape[1]] = vectors_ref[...]
    vbuf[at.c, at.own, at.z] = vpad[...].astype(bf16)
    pl.semaphore_wait(barrier, len(friends))
    swaps = []
    for index, (low, high) in enumerate(((0, groups), (groups, slots))):
        swaps.append(
            remote(
                give_out.at[low:high], asm.at[low:high, my_rows, :],
                swap_s.at[index], swap_r.at[index], at.core,
            )
        )
    swaps.append(
        remote(wdown_ref.at[:, other], asm_down.at[my_tall, :], swap_s.at[2], swap_r.at[2], at.core)
    )
    for swap in swaps:
        swap.start()
    for slot in range(slots):
        lane = 0
        for piece in own_slot(slot, at.c, mine):
            asm[slot, my_rows, lane : lane + piece.shape[1]] = piece
            lane += piece.shape[1]
    asm_down[my_tall, :] = wdown_ref[:, mine]

    def weight_piece(block, z, place, own_half):
        side = at.c if own_half else 1 - at.c
        if z is None:
            return w.at[block, side, place]
        return w.at[block, side, place, z]

    def vector_piece(block, z, place, own_half):
        core = at.c if own_half else 1 - at.c
        if z is None:
            return vbuf.at[core, place]
        return vbuf.at[core, place, z]

    def plane(block):
        after = block - groups
        if isinstance(block, int):
            return after > 0 and after % 2 == 0, after // 2 - 1
        return jnp.logical_and(after > 0, lax.rem(after, 2) == 0), after // 2 - 1

    weights = Gather(at, weight_piece, ag_s, ag_r, plane)
    vectors = Gather(at, vector_piece, vg_s, vg_r)

    def push(block):
        def every():
            slot = jnp.where(block > groups, groups + 1 + (block - groups - 1) // 2, block)
            w[block, at.c, at.own, at.z] = asm[slot].astype(bf16)

        def one(z):
            @pl.when(at.z == z)
            def _():
                w[block, at.c, at.own] = asm_down[...].reshape(depth, slab, half).astype(bf16)

        weights.split(block, every, one)
        weights.push(block)

    def gather_even(turn):
        last, block = turn - 3, turn
        when(both(last >= 0, last < blocks), lambda: weights.stage_four(last))

        when(block < blocks, lambda: weights.stage_two(block))

    def gather_odd(turn):
        block = turn - 1
        when(both(block >= 0, block < blocks), lambda: weights.stage_three(block))

    vectors.push(0)
    swaps[0].wait_recv()
    for block in range(groups):
        push(block)
    mark_segments(ends_ref, key_seg, query_seg)
    swaps[1].wait_recv()
    swaps[2].wait_recv()
    vectors.stage_two(0)
    gather_even(0)
    for block in range(groups, 2 * groups):
        push(block)
    vectors.stage_three(0)
    gather_even(1)
    gather_odd(1)
    for block in range(2 * groups, blocks):
        push(block)
    vectors.stage_four(0)
    gather_even(2)
    gather_odd(2)
    vectors.finish(0)
    gather_even(3)

    per = vectors_ref.shape[1]
    lane_inverse = (1 << 16) // per + 1
    spread_row = lax.broadcasted_iota(jnp.int32, (128, width), 0)
    spread_col = lax.broadcasted_iota(jnp.int32, (128, width), 1)
    spread_place = spread_col - ((spread_col * lane_inverse) >> 16) * per
    spread = jnp.where(spread_row == spread_place, 1.0, 0.0).astype(bf16)
    whole = jnp.zeros((16, width), f32)
    row = lax.broadcasted_iota(jnp.int32, (8 * 16, width), 0)
    col = (lax.broadcasted_iota(jnp.int32, (8 * 16, width), 1) * lane_inverse) >> 16
    core, place = row >> 6, (row >> 4) & 3
    place = jnp.where(core == 0, ((place & 1) << 1) | (place >> 1), place)
    device = place * 2 + core
    for level in range(depth):
        values = dot(vbuf[:, :, level].reshape(8 * 16, 128), spread)
        values = jnp.where(col == device + level * 8, values, 0.0).reshape(8, 16, width)
        whole = whole + jnp.sum(values, 0)
    vec[...] = whole

    def first_norm(target, first_time):
        @pl.loop(0, rows // ROWS)
        def _(step):
            here = rows_at(step)
            value = dy[here, :].astype(f32)
            unit, _ = standardize(value)
            hidden = (unit * vec[0:1, :] + vec[1:2, :]).astype(bf16)
            if first_time:
                target[here, :] = hidden
                middle[here, :] = value
            else:
                target[:, here] = hidden.T

    load_x.wait()
    first_norm(act, True)
    load_dy = pltpu.make_async_copy(cot_hbm, dy, local_s.at[0])
    load_dy.start()

    third = 3 * PAIR

    def group_columns(group, offset, count):
        return pl.ds(pl.multiple_of(group * width + offset, 128), count)

    def lane_of(part, side):
        return side * third + (part - side) % 3 * PAIR

    def q_at(group, side):
        return group_columns(group, lane_of(0, side), PAIR)

    def k_at(group, side):
        return group_columns(group, lane_of(1, side), PAIR)

    def v_at(group, side):
        return group_columns(group, lane_of(2, side), PAIR)

    def kv_at(group, side):
        return group_columns(group, lane_of(1, side), 2 * PAIR)

    def far_columns(group, side):
        return pl.ds(pl.multiple_of((2 * group + side) * 2 * PAIR, 128), 2 * PAIR)

    y_blk, core_blk = (1 - at.y) * 2 + at.c, at.y * 2 + 1 - at.c
    both_blk = 3 - at.blk

    def keys_copy(group, role, incoming=False):
        columns = pl.ds(pl.multiple_of(group * 4 * PAIR, 128), 4 * PAIR)
        device = (at.y_peer, at.core, at.core)[role]
        if incoming:
            source = target = far.at[(y_blk, core_blk, both_blk)[role], :, columns]
        elif role == 2:
            source = target = far.at[y_blk, :, columns]
        else:
            source = qkv.at[SHORT_DEV:, group_columns(group, PAIR, 4 * PAIR)]
            target = far.at[at.blk, :, columns]
        return remote(source, target, kv_s.at[group, role], kv_r.at[group, role], device)

    def strips(natural):
        for side in range(2):
            for place in range(4):
                high, low = place // 2, place % 2
                chip = (low * 2 + high) if side == 0 else place
                for level in range(depth):
                    order = chip * depth + level if natural else level * 4 + chip
                    yield side, place, level, order * slab

    def flatten(target, block, natural=False):
        for side, place, level, start in strips(natural):
            target[start : start + slab, side * half : (side + 1) * half] = w[
                block, side, place, level
            ]

    @pl.loop(0, groups)
    def _(group):
        weights.finish(group)
        bias = []
        for side in range(2):
            lanes = pl.ds(pl.multiple_of((2 * group + side) * PAIR, PAIR), PAIR)
            three = [vec[4:5, lanes], jnp.zeros((1, PAIR), f32), vec[5:6, lanes]]
            bias += three[side:] + three[:side]
        flat_down[0:1, :] = jnp.concatenate(bias, 1).astype(bf16)
        flatten(flat_up, group)

        @pl.loop(0, width // wide)
        def _(step):
            made = dot(act[...], flat_up[:, wide_at(step)])
            made = made + flat_down[0:1, wide_at(step)].astype(f32)
            qkv[:, group_columns(group, step * wide, wide)] = made.astype(bf16)

        keys_copy(group, 0).start()
        keys_copy(group, 1).start()
        for side in range(2):
            far[at.blk, :, far_columns(group, side)] = qkv[SHORT_DEV:, kv_at(group, side)]
            turned[side * PAIR : (side + 1) * PAIR, :] = qkv[:SHORT_DEV, v_at(group, side)].T

        gather_odd(groups + 2 * group)

        def tile_rows(tile):
            return pl.ds(pl.multiple_of(tile * TILE, TILE), TILE)

        def slot_rows(slot):
            return slice(slot * BAND, (slot + 1) * BAND)

        def products(tile, side):
            made = unstack_heads(
                dot(
                    turned[side * PAIR : (side + 1) * PAIR, pl.ds(band_start(tile), BAND)],
                    flat_down[slot_rows(side), :wide],
                )
            )
            att[pair_lanes(group * 2 + side), tile_rows(tile)] = made.astype(bf16)

        def soften(tile, side):
            allowed = short_mask(tile, key_seg, query_seg)
            probs, log_total = softmax_of(out_acc[slot_rows(side), :wide], allowed)
            flat_down[slot_rows(side), :wide] = probs
            lse[tile, group * 2 + side] = log_total

        def compare(tile, side):
            queries = stack_heads(qkv[tile_rows(tile), q_at(group, side)], score_scale)
            keys = qkv[pl.ds(band_start(tile), BAND), k_at(group, side)]
            out_acc[slot_rows(side), :wide] = dot_tr(keys, queries)

        @pl.loop(0, tiles + 1)
        def _(turn):
            now, last = jnp.minimum(turn, tiles - 1), jnp.maximum(turn - 1, 0)
            products(last, 0)
            soften(last, 1)
            compare(now, 0)
            products(last, 1)
            soften(now, 0)
            compare(now, 1)
            pl.when(turn == 1)(lambda: gather_even(groups + 1 + 2 * group))

            @pl.when(turn == 3)
            def _():
                gather_odd(groups + 1 + 2 * group)
                keys_copy(group, 0, True).wait_recv()
                keys_copy(group, 2).start()

            pl.when(turn == 6)(lambda: gather_even(groups + 2 + 2 * group))

    def far_pair(pair, offset):
        return pl.ds(pl.multiple_of(pair * 2 * PAIR + offset, PAIR), PAIR)

    def far_block(pair, offset):
        return far[:, :, far_pair(pair, offset)].reshape(4 * LONG_DEV, PAIR)

    gather_odd(3 * groups)
    for group in range(groups):
        keys_copy(group, 1, True).wait_recv()
        keys_copy(group, 2, True).wait_recv()

    @pl.loop(0, groups)
    def _(group):
        allowed = long_mask(length_ref, 4 * LONG_DEV)
        for side in range(2):
            pair = 2 * group + side
            made, log_total = attend_forward(
                qkv[SHORT_DEV:, q_at(group, side)],
                far_block(pair, 0),
                far_block(pair, PAIR).T,
                allowed,
            )
            att[pair_lanes(pair), SHORT_DEV:] = made
            lse[tiles, pair] = log_total
        pl.when(group == 0)(lambda: gather_even(3 * groups + 1))
        pl.when(group == groups - 1)(lambda: gather_odd(3 * groups + 1))

    weights.finish(groups)
    for group in range(groups):
        for role in range(3):
            keys_copy(group, role).wait_send()

    load_dy.wait()
    place = lax.broadcasted_iota(jnp.int32, (LONG_DEV, width), 0) + at.blk * LONG_DEV
    keep = place < length_ref[0]
    dy[SHORT_DEV:, :] = jnp.where(keep, dy[SHORT_DEV:, :].astype(f32), 0.0).astype(bf16)

    act[...] = att[...].T
    flatten(flat_up, groups)
    gather_even(3 * groups + 2)

    @pl.loop(0, width // wide)
    def _(step):
        columns = wide_at(step)
        made = dot(act[...], flat_up[:, columns]) + vec[6:7, columns]
        middle[:, columns] = middle[:, columns] + made

    @pl.loop(0, rows // ROWS)
    def _(step):
        here = rows_at(step)
        unit, _ = standardize(middle[here, :])
        hidden = (unit * vec[2:3, :] + vec[3:4, :]).astype(bf16)
        h2[here, :] = hidden
        h2_tr[:, here] = hidden.T

    def piece(block, place):
        return w.at[block, at.c, place]

    turns = [*range(groups + 1, blocks), groups, *range(groups)]

    def landing(block, side):
        if isinstance(block, int) and block <= groups:
            return turns[turns.index(block) - 4], side
        order = block - groups - 1
        odd = jnp.logical_and(order < 4, lax.rem(order, 2) == 1)
        return (
            jnp.where(order < 4, spare + order // 2, block - 4),
            jnp.where(odd, 1 - side, side),
        )

    def to_core(block):
        place, side = landing(block, at.c)
        return remote(
            w.at[block, 1 - at.c], w.at[place, side], rs_s.at[block, 0], rs_r.at[block, 0], at.core
        )

    def going(block, index):
        sends, recvs = rs_s.at[block, index], rs_r.at[block, index]
        if index == 1:
            return remote(piece(block, at.far_two), got_a.at[block], sends, recvs, at.second)
        return remote(piece(block, at.at_first), got_b.at[block], sends, recvs, at.first)

    def along_z(block, step):
        index = 4 + step
        return remote(
            w.at[block, at.c, at.own, at.z_to(step)], got_z.at[block, step - 1],
            rs_s.at[block, index], rs_r.at[block, index], at.z_peer(step),
        )

    def to_plane(block, step):
        index = 4 + step
        return remote(
            piece(block, at.own), got_zd.at[step - 1],
            rs_s.at[block, index], rs_r.at[block, index], at.z_peer(step),
        )

    def swap_back(block, tall_one, incoming=False):
        sends, recvs = rs_s.at[block, 4], rs_r.at[block, 4]
        columns = other if incoming else mine
        if tall_one:
            return remote(
                asm_down.at[other_tall, :], red.at[pl.ds(blocks_low, tall), columns],
                sends, recvs, at.core,
            )
        return remote(
            asm.at[slot_of(block), other_rows, :], red.at[red_rows(block), columns],
            sends, recvs, at.core,
        )

    blocks_low = slots * share

    def slot_of(block):
        if isinstance(block, int):
            return block if block <= groups else groups + 1 + (block - groups - 1) // 2
        return jnp.where(block > groups, groups + 1 + (block - groups - 1) // 2, block)

    def red_rows(block):
        return pl.ds(pl.multiple_of(slot_of(block) * share, 8), share)

    def add_piece(block, place, got):
        w[block, at.c, place] = w[block, at.c, place] + got

    def scatter_one(block):
        to_core(block).wait_recv()
        where, side = landing(block, 1 - at.c)
        add_piece(block, at.far_two, w[where, side, at.far_two])
        going(block, 1).start()
        add_piece(block, at.near_two, w[where, side, at.near_two])

    def scatter_two(block):
        going(block, 1).wait_recv()
        add_piece(block, at.at_first, got_a[block, 1 - at.f])
        going(block, 3).start()
        add_piece(block, at.own, got_a[block, at.f])

    def scatter_three(block):
        going(block, 3).wait_recv()
        add_piece(block, at.own, got_b[block])

        def every():
            for step in range(1, depth):
                along_z(block, step).start()

        def one(z):
            @pl.when(at.z != z)
            def _():
                to_plane(block, lax.rem(z - at.z + depth, depth)).start()

        weights.split(block, every, one)

    def scatter_four(block):
        def every():
            total = w[block, at.c, at.own, at.z].astype(f32)
            for step in range(1, depth):
                along_z(block, step).wait_recv()
                total = total + got_z[block, step - 1].astype(f32)
            slot = slot_of(block)
            asm[slot] = total
            squares[...] += total * total
            swap_back(block, False).start()
            red[red_rows(block), mine] = asm[slot, my_rows, :]

        def one(z):
            @pl.when(at.z == z)
            def _():
                for step in range(1, depth):
                    to_plane(block, step).wait_recv()
                total = w[block, at.c, at.own].astype(f32)
                for step in range(1, depth):
                    total = total + got_zd[step - 1].astype(f32)
                asm_down[...] = total.reshape(2 * tall, half)
                squares[...] += jnp.sum(total * total, 0)
                swap_back(block, True).start()
                red[pl.ds(blocks_low, tall), mine] = asm_down[my_tall, :]

        weights.split(block, every, one)

    def scatter_end(block):
        def every():
            swap_back(block, False, True).wait_recv()
            swap_back(block, False).wait_send()
            for step in range(1, depth):
                along_z(block, step).wait_send()

        def one(z):
            @pl.when(at.z == z)
            def _():
                swap_back(block, True, True).wait_recv()
                swap_back(block, True).wait_send()

            @pl.when(at.z != z)
            def _():
                to_plane(block, lax.rem(z - at.z + depth, depth)).wait_send()

        weights.split(block, every, one)
        for index in (1, 3):
            going(block, index).wait_send()

    stages = (scatter_one, scatter_two, scatter_three, scatter_four)

    def scatter_pump(turn):
        for stage, first, pace in zip(stages, (4, 7, 11, 14), (2, 3, 3, 3)):
            if isinstance(turn, int):
                order = (turn - first) // pace
                if (turn - first) % pace == 0 and 0 <= order <= 2 * units:
                    stage(turns[order])
                continue
            late = turn - first
            due = jnp.logical_and(late >= 0, lax.rem(late, pace) == 0)
            pl.when(due)(functools.partial(stage, groups + 1 + lax.div(late, pace)))

    def give(block, gradient, natural=False):
        weights.sent(block)
        if isinstance(block, int) and block <= groups:
            to_core(turns[turns.index(block) - 2]).wait_send()
        else:
            pl.when(block > groups + 2)(lambda: to_core(block - 2).wait_send())
        low = gradient.astype(bf16)
        for side, place, level, start in strips(natural):
            w[block, side, place, level] = low[
                start : start + slab, side * half : (side + 1) * half
            ]
        to_core(block).start()

    squares[...] = jnp.zeros_like(squares)
    out_acc[...] = jnp.zeros_like(out_acc)
    dh2[...] = jnp.zeros_like(dh2)
    gvec[...] = jnp.zeros_like(gvec)

    @pl.loop(0, units)
    def _(unit):
        up, down = groups + 1 + 2 * unit, groups + 2 + 2 * unit
        weights.finish(up)
        weights.finish(down)
        flatten(flat_up, up)
        flatten(flat_down, down, True)

        @pl.loop(0, width // wide)
        def _(step):
            @pl.when(step == 0)
            def _():
                gather_odd(3 * groups + 2 + 2 * unit)
                scatter_pump(4 * unit)

            @pl.when(step == 2)
            def _():
                gather_even(3 * groups + 3 + 2 * unit)
                scatter_pump(4 * unit + 1)

            columns = wide_at(step)
            pre = dot(h2[...], flat_up[:, columns]) + vec[pl.ds(8 + unit, 1), columns]
            grad_act = dot_tr(dy[...], flat_down[columns, :])
            made, slope = gelu_both(pre)
            act[:, columns] = made.astype(bf16)
            du_low = (grad_act * slope).astype(bf16)
            du[:, columns] = du_low
            gvec[pl.ds(8 + unit, 1), columns] = column_sum(du_low.astype(f32))

        @pl.loop(0, width // wide)
        def _(step):
            @pl.when(step == 1)
            def _():
                gather_odd(3 * groups + 3 + 2 * unit)
                scatter_pump(4 * unit + 2)

            columns = wide_at(step)
            out_acc[:, columns] += dot(act[...], flat_down[:, columns])
            dh2[:, columns] += dot_tr(du[...], flat_up[columns, :])

        gather_even(3 * groups + 4 + 2 * unit)
        scatter_pump(4 * unit + 3)
        give(up, dot(h2_tr[...], du[...]))
        give(down, dot_tl(act[...], dy[...]), True)

    def body(step, totals):
        here = rows_at(step)
        for turn in range(rows // ROWS):
            pl.when(step == turn)(functools.partial(scatter_pump, 4 * units + turn))
        middle_here = middle[here, :]
        out = middle_here + (out_acc[here, :] + vec[7:8, :])
        h2[here, :] = out.astype(bf16)
        dy_here = dy[here, :].astype(f32)
        dh2_here = dh2[here, :]
        unit, inv_std = standardize(middle_here)
        dmiddle = dy_here + norm_back(dh2_here, unit, inv_std, vec[2:3, :])
        dh2[here, :] = dmiddle
        da = dmiddle.astype(bf16)
        act[here, :] = da
        return (
            totals[0] + column_sum(dh2_here * unit),
            totals[1] + column_sum(dh2_here),
            totals[2] + column_sum(da.astype(f32)),
            totals[3] + column_sum(dy_here),
        )

    zero = jnp.zeros((1, width), f32)
    sums = lax.fori_loop(0, rows // ROWS, body, (zero,) * 4)
    flatten(flat_up, groups)

    @pl.loop(0, width // wide)
    def _(step):
        columns = wide_at(step)
        du[:, columns] = dot_tr(act[...], flat_up[columns, :]).astype(bf16)

    for place, total in zip((2, 3, 6, 7), sums):
        gvec[place : place + 1, :] = total
    store_out = pltpu.make_async_copy(h2, out_hbm, local_s.at[0])
    store_out.start()
    load_again = pltpu.make_async_copy(x_hbm, dy, local_s.at[2])
    load_again.start()
    give(groups, dot(att[...], act[...]))
    load_again.wait()
    first_norm(h2_tr, False)

    after = 4 * units + rows // ROWS

    @pl.loop(0, groups)
    def _(group):
        allowed = long_mask(length_ref, 4 * LONG_DEV)
        for side in range(2):
            pair = 2 * group + side
            dq, dk, dv = attend_back(
                qkv[SHORT_DEV:, q_at(group, side)],
                far_block(pair, 0),
                far_block(pair, 0).T,
                far_block(pair, PAIR),
                allowed,
                lse[tiles, pair],
                du[SHORT_DEV:, pair_lanes(pair)],
            )
            qkv[SHORT_DEV:, q_at(group, side)] = dq
            far[:, :, far_pair(pair, 0)] = dk.astype(bf16).reshape(4, LONG_DEV, PAIR)
            far[:, :, far_pair(pair, PAIR)] = dv.astype(bf16).reshape(4, LONG_DEV, PAIR)
        for turn in range(groups):
            pl.when(group == turn)(functools.partial(scatter_pump, after + turn))

    flats = (flat_up, act.at[:width, :], att.at[:, :width])

    far_one = remote(far.at[core_blk], far_got.at[0], fg_s.at[0], fg_r.at[0], at.core)
    far_two = remote(far.at[both_blk], far_got.at[1], fg_s.at[1], fg_r.at[1], at.core)
    far_three = remote(far.at[y_blk], far_got.at[2], fg_s.at[2], fg_r.at[2], at.y_peer)
    far_two.start()
    far_one.start()
    store_out.wait()
    lse[tiles + 1] = jnp.full(lse.shape[1:], 1e30, f32)
    flat_down[...] = jnp.zeros_like(flat_down)

    @pl.loop(0, groups)
    def _(group):
        middle[:SHORT_DEV, 0 : 4 * PAIR] = jnp.zeros((SHORT_DEV, 4 * PAIR), f32)
        flat_down[:BAND, 0 : 2 * wide] = jnp.zeros((BAND, 2 * wide), bf16)
        before = group - 1

        def pump(place):
            for now in range(groups):
                turn = after + groups + 5 * now + place
                pl.when(group == now)(functools.partial(scatter_pump, turn))

            @pl.when(group > 0)
            def _():
                if place == 0:
                    pl.when(group > 1)(lambda: scatter_four(group - 2))
                if place == 1:
                    for block in range(groups - 1):
                        pl.when(before == block)(functools.partial(scatter_one, block))
                if place == 3:
                    scatter_two(before)
                if place == 4:
                    scatter_three(before)

        pump(0)
        for side in range(2):
            turned[side * PAIR : (side + 1) * PAIR, :] = qkv[:SHORT_DEV, k_at(group, side)].T

        def tile_rows(tile):
            return pl.ds(pl.multiple_of(tile * TILE, TILE), TILE)

        def slot_rows(slot):
            return slice(slot * BAND, (slot + 1) * BAND)

        def stacked(tile, side):
            here = tile_rows(tile)
            return (
                stack_heads(qkv[here, q_at(group, side)], score_scale),
                stack_heads(du[here, pair_lanes(group * 2 + side)], None),
            )

        def products(tile, side, target):
            queries, upstream = stacked(tile, side)
            band = pl.ds(band_start(tile), BAND)
            probs = flat_down[slot_rows(side), :wide]
            grad_scores = flat_down[slot_rows(side), wide : 2 * wide]
            start = side * 2 * PAIR
            middle[band, start : start + PAIR] += dot(grad_scores, queries)
            middle[band, start + PAIR : start + 2 * PAIR] += dot(probs, upstream)
            keys_tr = turned[side * PAIR : (side + 1) * PAIR, band]
            dq = unstack_heads(dot(keys_tr, grad_scores)) * score_scale
            h2[tile_rows(target), pair_lanes(group * 2 + side)] = dq.astype(bf16).T

        def soften(tile, side, source):
            allowed = short_mask(tile, key_seg, query_seg)
            probs, grad_scores = softmax_back(
                middle[slot_rows(side), 2 * wide : 3 * wide],
                allowed,
                lse[source, group * 2 + side],
                out_acc[slot_rows(side), :wide],
            )
            flat_down[slot_rows(side), :wide] = probs
            flat_down[slot_rows(side), wide : 2 * wide] = grad_scores

        def compare(tile, side):
            queries, upstream = stacked(tile, side)
            band = pl.ds(band_start(tile), BAND)
            middle[slot_rows(side), 2 * wide : 3 * wide] = dot_tr(
                qkv[band, k_at(group, side)], queries
            )
            out_acc[slot_rows(side), :wide] = dot_tr(qkv[band, v_at(group, side)], upstream)

        @pl.loop(0, tiles + 1)
        def _(turn):
            now, last = jnp.minimum(turn, tiles - 1), jnp.maximum(turn - 1, 0)
            target = jnp.where(turn == 0, tiles, last)
            products(last, 0, target)
            soften(last, 1, jnp.where(turn == 0, tiles + 1, last))
            compare(now, 0)
            products(last, 1, target)
            soften(now, 0, now)
            compare(now, 1)

            @pl.when(turn == 1)
            def _():
                pump(1)

                @pl.when(group == 0)
                def _():
                    far_two.wait_recv()
                    far[y_blk] = far[y_blk] + far_got[1]
                    far_three.start()

            pl.when(turn == 3)(lambda: pump(2))
            pl.when(turn == 6)(lambda: pump(3))

        for side in range(2):
            qkv[:SHORT_DEV, q_at(group, side)] = h2[:SHORT_DEV, pair_lanes(group * 2 + side)]

        @pl.when(group == 0)
        def _():
            far_one.wait_recv()
            far_three.wait_recv()

        for side in range(2):
            start = side * 2 * PAIR
            qkv[:SHORT_DEV, kv_at(group, side)] = middle[
                :SHORT_DEV, start : start + 2 * PAIR
            ].astype(bf16)
            near_at = far_columns(group, side)
            near = far[at.blk, :, near_at].astype(f32) + far_got[0, :, near_at].astype(f32)
            near = near + far_got[2, :, near_at].astype(f32)
            qkv[SHORT_DEV:, kv_at(group, side)] = near.astype(bf16)

        for block, target in enumerate(flats):
            pl.when(group == block)(functools.partial(flatten, target, block))
        gradient = dot(h2_tr[...], qkv[:, group_columns(group, 0, width)])
        for block in range(groups):
            pl.when(group == block)(functools.partial(give, block, gradient))

        pump(4)
        sums = column_sum(qkv[:, group_columns(group, 0, width)].astype(f32))
        for side in range(2):
            own = pl.ds(pl.multiple_of((2 * group + side) * PAIR, PAIR), PAIR)
            for part, line in ((0, 4), (2, 5)):
                lane = lane_of(part, side)
                gvec[line : line + 1, own] = sums[:, lane : lane + PAIR]

    def input_rows(step):
        here = pl.ds(step * (rows // 2), rows // 2)
        unit, inv_std = standardize(dy[here, :].astype(f32))
        dh1 = out_acc[here, :]
        middle[here, :] = dh2[here, :] + norm_back(dh1, unit, inv_std, vec[0:1, :])
        return column_sum(dh1 * unit), column_sum(dh1)

    latest = groups - 1
    scatter_one(latest)

    @pl.loop(0, width // wide)
    def _(step):
        columns = wide_at(step)
        made = jnp.zeros((rows, wide), f32)
        for group, flat in enumerate(flats):
            made = made + dot_tr(qkv[:, group * width : (group + 1) * width], flat[columns, :])
        out_acc[:, columns] = made

    gain_low, shift_low = input_rows(0)
    scatter_pump(after + 6 * groups)
    scatter_four(latest - 1)
    gain_high, shift_high = input_rows(1)
    store_grad = pltpu.make_async_copy(middle, grad_hbm, local_s.at[1])
    store_grad.start()
    gvec[0:1, :] = gain_low + gain_high
    gvec[1:2, :] = shift_low + shift_high
    exchange = Exchange(at, v_sent, v_got, v_got_z, ex_s, ex_r, 0)
    exchange.begin(gvec[...])
    scatter_two(latest)
    exchange.step()
    scatter_three(latest)
    exchange.step()
    exchange.step()
    scatter_four(latest)

    weight_square = jnp.sum(squares[...], keepdims=True)
    norms = ShortExchange(at, n_sent, n_got_z, n_got, no_s, no_r)
    norm_copies = norms.along_z(jnp.broadcast_to(weight_square, n_sent.shape[1:]))
    vector_sum = exchange.step()
    device = at.dp * 4 + at.blk
    turn_by = lax.rem(width - device * per, width)
    rvec_ref[...] = pltpu.roll(vector_sum, turn_by, 1)[:, :128]
    vector_square = jnp.sum(vector_sum * vector_sum, keepdims=True)
    norm_copies = norms.in_plane(norms.finish(n_got_z, norm_copies))

    @pl.loop(0, blocks)
    def _(block):
        @pl.when(block > groups)
        def _():
            scatter_end(block)

    for block in range(groups + 1):
        scatter_end(block)
    for block in turns[-2:]:
        to_core(block).wait_send()
    for group in range(groups):
        for side in range(2):
            for part in range(3):
                start = part * width + (2 * group + side) * PAIR
                lane = lane_of(part, side)
                rqkv_ref[:, start : start + PAIR] = red[
                    group * share : (group + 1) * share, lane : lane + PAIR
                ]
    rout_ref[...] = red[groups * share : (groups + 1) * share, :]
    for unit in range(units):
        start = (groups + 1 + unit) * share
        rup_ref[:, unit * width : (unit + 1) * width] = red[start : start + share, :]
    rdown_ref[...] = red[blocks_low : blocks_low + tall, :]
    far_one.wait_send()
    far_two.wait_send()
    far_three.wait_send()
    for swap in swaps:
        swap.wait_send()
    vectors.sent(0)
    norm_ref[...] = jnp.sqrt(norms.finish(n_got, norm_copies) + vector_square)
    store_grad.wait()


def run_fused(depth, patches, cotangent, ends, length, w_qkv, w_out, w_up, w_down, vectors):
    rows, width = patches.shape
    share = w_out.shape[0]
    tall = w_down.shape[0]
    bf16, f32 = jnp.bfloat16, jnp.float32
    slab = 2 * share
    lanes4 = 2 * PAIR
    groups = width // lanes4
    units = w_up.shape[1] // width
    slots = groups + 1 + units
    blocks = slots + units
    half = width // 2
    tiles = SHORT_DEV // TILE
    vmem = lambda shape, kind: pltpu.VMEM(shape, kind)
    dma = pltpu.SemaphoreType.DMA
    copies = depth + 3
    scratch = [
        vmem((blocks + 2, 2, 4, depth, slab, half), bf16),
        vmem((2, 4, depth, 16, 128), bf16),
        vmem((16, 128), f32),
        vmem((slots, share, half), f32),
        vmem((slots, slab, half), f32),
        vmem((2 * tall, half), f32),
        vmem((16, width), f32),
        vmem((rows, 3 * width), bf16),
        vmem((width, rows), bf16),
        vmem((rows, width), f32),
        vmem((rows, width), bf16),
        vmem((rows, width), bf16),
        vmem((rows, width), bf16),
        vmem((rows, width), f32),
        vmem((rows, width), f32),
        vmem((rows, width), bf16),
        vmem((4, LONG_DEV, 2 * width), bf16),
        vmem((3, LONG_DEV, 2 * width), bf16),
        vmem((tiles + 2, width // PAIR, 1, 2 * TILE), f32),
        vmem((SHORT_DEV, TILE), f32),
        vmem((tiles, 1, TILE), f32),
        vmem((lanes4, SHORT_DEV), bf16),
        vmem((width, rows), bf16),
        vmem((width, width), bf16),
        vmem((width, width), bf16),
        vmem((blocks, 2, depth, slab, half), bf16),
        vmem((blocks, depth, slab, half), bf16),
        vmem((blocks, depth - 1, slab, half), bf16),
        vmem((depth - 1, depth, slab, half), bf16),
        vmem((slots * share + tall, width), f32),
        vmem((slab, half), f32),
        vmem((16, width), f32),
        vmem((4, 16, width), f32),
        vmem((3, 16, width), f32),
        vmem((depth, 16, width), f32),
        vmem((2, 8, 128), f32),
        vmem((8, 8, 128), f32),
        vmem((depth, 8, 128), f32),
    ]
    scratch += [dma((3,))] * 2 + [dma((blocks, copies))] * 2 + [dma((1, copies))] * 2
    scratch += [dma((groups, 3))] * 2 + [dma((3,))] * 2 + [dma((blocks, 4 + depth))] * 2
    scratch += [dma((1, 3 + depth))] * 2 + [dma((depth + 6,))] * 2 + [dma((3,))]
    in_vmem = pl.BlockSpec(memory_space=pltpu.VMEM)
    in_smem = pl.BlockSpec(memory_space=pltpu.SMEM)
    anywhere = pl.BlockSpec(memory_space=pl.ANY)
    return pl.pallas_call(
        functools.partial(fused_kernel, depth),
        out_shape=[
            jax.ShapeDtypeStruct((rows, width), bf16),
            jax.ShapeDtypeStruct((rows, width), f32),
            jax.ShapeDtypeStruct(w_qkv.shape, f32),
            jax.ShapeDtypeStruct(w_out.shape, f32),
            jax.ShapeDtypeStruct(w_up.shape, f32),
            jax.ShapeDtypeStruct(w_down.shape, f32),
            jax.ShapeDtypeStruct((16, 128), f32),
            jax.ShapeDtypeStruct((8, 128), f32),
        ],
        in_specs=[in_smem] * 2 + [in_vmem] * 5 + [anywhere] * 2,
        out_specs=[anywhere] * 2 + [in_vmem] * 6,
        scratch_shapes=scratch,
        compiler_params=pltpu.CompilerParams(
            vmem_limit_bytes=FUSED_VMEM, collective_id=0, has_side_effects=True
        ),
    )(ends, length, w_qkv, w_out, w_up, w_down, vectors, patches, cotangent)


def adamw_kernel(*refs):
    out_in, grad_in, norm_ref, out_out, grad_out, total_ref = *refs[:3], *refs[23:26]
    sources = [refs[3 + 5 * kind : 8 + 5 * kind] for kind in range(4)]
    targets = [refs[26 + 5 * kind : 31 + 5 * kind] for kind in range(4)]
    through, sems = refs[46:48], refs[48]
    loads, stores = [], []
    for place, (source, target) in enumerate(((out_in, out_out), (grad_in, grad_out))):
        loads.append(pltpu.make_async_copy(source, through[place], sems.at[place]))
        stores.append(pltpu.make_async_copy(through[place], target, sems.at[2 + place]))
    for load in loads:
        load.start()
    total_ref[...] = norm_ref[0:1, 0:1]
    factor = 1.0 / jnp.maximum(norm_ref[0:1, 0:1], 1.0)
    for load, store in zip(loads, stores):
        load.wait()
        store.start()
    for place in range(5):
        weight, first, second, gradient = (source[place] for source in sources)
        rate, decay = (rate_vector, 0.0) if place == 4 else (rate_matrix, decay_weight)
        lines, columns = weight.shape
        new = adamw_step(
            weight[...], gradient[:lines, :columns] * factor, first[...], second[...], rate, decay
        )
        for target, value in zip(targets, (*new, new[0])):
            target[place][...] = value.astype(target[place].dtype)
    for store in stores:
        store.wait()


def run_adamw(result, input_grad, norm, weights, firsts, seconds, gradients):
    f32 = jnp.float32
    outs = [jax.ShapeDtypeStruct(part.shape, part.dtype) for part in (result, input_grad)]
    outs.append(jax.ShapeDtypeStruct((1, 1), f32))
    for kind in (f32, f32, f32, jnp.bfloat16):
        outs += [jax.ShapeDtypeStruct(part.shape, kind) for part in weights]
    in_vmem, anywhere = pl.BlockSpec(memory_space=pltpu.VMEM), pl.BlockSpec(memory_space=pl.ANY)
    found = pl.pallas_call(
        adamw_kernel,
        out_shape=outs,
        in_specs=[anywhere] * 2 + [in_vmem] * 21,
        out_specs=[anywhere] * 2 + [in_vmem] * 21,
        scratch_shapes=[
            pltpu.VMEM(result.shape, result.dtype),
            pltpu.VMEM(input_grad.shape, input_grad.dtype),
            pltpu.SemaphoreType.DMA((4,)),
        ],
        compiler_params=pltpu.CompilerParams(vmem_limit_bytes=VMEM_MOST),
    )(result, input_grad, norm, *weights, *firsts, *seconds, *gradients)
    return found[0], found[1], found[2].reshape(()), *found[3:]


def adamw_step(weight, gradient, first_moment, second_moment, rate, decay):
    first_new = beta_first * first_moment + (1.0 - beta_first) * gradient
    second_new = beta_second * second_moment + (1.0 - beta_second) * gradient * gradient
    first_hat = first_new / (1.0 - beta_first**STEP)
    second_hat = second_new / (1.0 - beta_second**STEP)
    weight_new = weight - rate * (first_hat / (jnp.sqrt(second_hat) + eps_adam) + decay * weight)
    return (weight_new, first_new, second_new)


def gather_parameters(weights, vectors):
    low = [w.astype(jnp.bfloat16) for w in weights] + [vectors.astype(jnp.bfloat16)]
    flat = jnp.concatenate([part.reshape(-1) for part in low])
    flat = jnp.pad(flat, (0, -flat.size % 4096)).reshape(-1, 128)
    whole = lax.all_gather(flat, ("dp", "blk"), axis=0, tiled=True)
    whole = whole.reshape(-1, flat.size)
    found, at = [], 0
    for part in low[:-1]:
        piece = whole[:, at : at + part.size]
        found.append(piece.reshape(-1, part.shape[1]))
        at += part.size
    piece = whole[:, at : at + vectors.size].reshape(-1, *vectors.shape)
    found.append(piece.transpose(1, 0, 2).reshape(vectors.shape[0], -1))
    return found


def layer_by_parts(
    patches, cotangent, short_lengths, long_lengths, w_qkv, w_out, w_up, w_down, vectors
):
    rows, width = patches.shape
    bf16, f32 = jnp.bfloat16, jnp.float32
    full_qkv, full_out, full_up, full_down, full_vec = gather_parameters(
        (w_qkv, w_out, w_up, w_down), vectors
    )
    params = full_vec.astype(f32)

    hidden_one, projected = call(
        qkv_phase, [((rows, width), bf16), ((rows, 3 * width), bf16)]
    )(patches, params, full_qkv)
    far = lax.all_gather(projected[SHORT_DEV:, width:], "blk", axis=0, tiled=True)
    tiles, pairs = SHORT_DEV // TILE, width // PAIR
    marks = [pltpu.VMEM((SHORT_DEV, TILE), f32), pltpu.VMEM((tiles, 1, TILE), f32)]
    attended, lse, middle, hidden_two = call(
        forward_kernel,
        [
            ((rows, width), bf16),
            ((tiles + 1, pairs, 1, 2 * TILE), f32),
            ((rows, width), f32),
            ((rows, width), bf16),
        ],
        scratch=marks,
        smem=(0, 1),
    )(short_lengths, long_lengths, patches, params, projected, far, full_out)

    long_place = lax.axis_index("blk") * LONG_DEV + jnp.arange(LONG_DEV, dtype=jnp.int32)
    keep = jnp.concatenate([jnp.ones((SHORT_DEV,), bool), long_place < long_lengths[0]])
    grad_low = jnp.where(keep[:, None], cotangent, jnp.zeros_like(cotangent))
    blocks = full_up.shape[1] // width
    result, grad_hidden_two, grad_up, grad_down, grad_bias_up = run_mlp(
        hidden_two, grad_low, middle, full_up, full_down,
        params[8 : 8 + blocks].reshape(blocks, 1, width), params[7:8],
    )
    scatter = functools.partial(
        lax.psum_scatter, axis_name=("dp", "blk"), scatter_dimension=0, tiled=True
    )
    red_up = scatter(grad_up)
    red_down = scatter(grad_down)

    grad_middle, grad_att, sums_two, grad_out = call(
        middle_back_kernel,
        [
            ((rows, width), f32),
            ((rows, width), bf16),
            ((4, width), f32),
            ((width, width), f32),
        ],
        scratch=[pltpu.VMEM((rows, width), bf16)],
    )(grad_low, middle, grad_hidden_two, params, full_out, attended)
    red_out = scatter(grad_out)

    mixed, far_grad = call(
        attention_back_kernel,
        [((rows, 3 * width), bf16), ((far.shape[0], 2 * width), bf16)],
        scratch=marks + [pltpu.VMEM((SHORT_DEV, 2 * PAIR), f32)] * 2,
        smem=(0, 1),
    )(short_lengths, long_lengths, projected, far, lse, grad_att)
    near = lax.psum_scatter(far_grad, "blk", scatter_dimension=0, tiled=True)
    input_grad, grad_qkv, sums_one = call(
        input_back_kernel,
        [((rows, width), f32), ((width, 3 * width), f32), ((4, width), f32)],
        scratch=[pltpu.VMEM((rows, 3 * width), bf16)],
    )(patches, hidden_one, mixed, near, params, full_qkv, grad_middle)
    red_qkv = scatter(grad_qkv)

    grad_vec = jnp.concatenate(
        [sums_one[0:2], sums_two[0:2], sums_one[2:4], sums_two[2:4], grad_bias_up.reshape(-1, width)], 0
    )
    red_vec = lax.psum_scatter(grad_vec, ("dp", "blk"), scatter_dimension=1, tiled=True)
    reduced = (red_qkv, red_out, red_up, red_down, red_vec)
    grad_norm = jnp.sqrt(
        lax.psum(sum(jnp.sum(part * part) for part in reduced), ("dp", "blk"))
    )
    return result, input_grad, grad_norm, reduced


def fits_one(patches, w_out):
    dp, blk = lax.axis_size("dp"), lax.axis_size("blk")
    share, width = w_out.shape
    return blk == 4 and dp % 2 == 0 and 2 * share % 16 == 0 and dp * blk * share == width


def per_device(
    patches, cotangent, short_lengths, long_lengths,
    w_qkv, w_out, w_up, w_down, vectors,
    first_qkv, first_out, first_up, first_down, first_vectors,
    second_qkv, second_out, second_up, second_down, second_vectors,
):
    layer = (patches, cotangent, short_lengths, long_lengths)
    weights = (w_qkv, w_out, w_up, w_down, vectors)
    if fits_one(patches, w_out):
        depth = lax.axis_size("dp") // 2
        result, input_grad, *gradients, norm = run_fused(depth, *layer, *weights)
    else:
        result, input_grad, grad_norm, gradients = layer_by_parts(*layer, *weights)
        norm = jnp.broadcast_to(grad_norm, (8, 128))
    firsts = (first_qkv, first_out, first_up, first_down, first_vectors)
    seconds = (second_qkv, second_out, second_up, second_down, second_vectors)
    return run_adamw(result, input_grad, norm, weights, firsts, seconds, gradients)


def solution(mesh):
    rows = P(("dp", "blk"), None)
    columns = P(None, ("dp", "blk"))
    group = (rows,) * 4 + (columns,)
    return jax.shard_map(
        per_device,
        mesh=mesh,
        in_specs=(rows, rows, rows, P("dp")) + group * 3,
        out_specs=(rows, rows, P()) + group * 4,
        check_vma=False,
    )
```

time: 981 us -> 233 us (0.24)
  waiting for transfers between devices: 449 us -> 0 us
  Pallas kernels: 0 us -> 231 us
  matrix products: 216 us -> 0 us
  blocking collectives: 142 us -> 0 us
  other arithmetic: 95.7 us -> 0 us
  local copies, waits for them, and re-layouts: 50 us -> 0 us
  between operations: 21 us -> 1.49 us
    reduce_scatter x4 -> x0, waiting for transfers between devices: 360 us -> none  [the longest x1 139 us: per_device(): lax.psum_scatter(grad_down, ('dp', 'blk'), scatter_dimension=0, tiled=True)]
    pallas_call x0 -> x2, Pallas kernels: none -> 231 us  [the longest x1 223 us: run_fused(): pl.pallas_call(functools.partial(fused_kernel, depth), out_shape=[jax.Sha...]
    dot_general x24 -> x0, matrix products: 216 us -> none  [the longest x4 36.1 us: outer_sum(): lax.dot_general(left_side, right_side, (((0,), (0,)), ((), ())), preferre...]
    all_gather x4 -> x0, waiting for transfers between devices: 88.4 us -> none  [the longest x1 54.7 us: per_device(): lax.all_gather(low_down, ('dp', 'blk'), axis=0, tiled=True)]
    all_gather x3 -> x0, blocking collectives: 62 us -> none  [the longest x1 43.7 us: per_device(): lax.all_gather(low_vec, ('dp', 'blk'), axis=1, tiled=True)]
    convert_element_type x11 -> x0, other arithmetic: 44.3 us -> none  [the longest x2 32.3 us: attend_back(): grad_scores = (attn_probs * (grad_probs - row_delta)).astype(jnp.bfloat16)]
    reduce_sum x15 -> x0, other arithmetic: 42.6 us -> none  [the longest x2 16.1 us: attend_forward(): row_total = jnp.sum(exponent, -1, keepdims=True)]
    unnamed x1 -> x0, blocking collectives: 40.5 us -> none
  transfers between devices with their start and end apart: 10 -> 0, of which waited for: 6 -> 0; matrix products, arithmetic and copies ran while one was open for 26% -> 0% of each run, Pallas kernels for 0% -> 0%
where the time goes in v1:
time: 233 us
  Pallas kernels  231 us (99%)
    pallas_call x1, Pallas kernels, run_fused(): pl.pallas_call(functools.partial(fused_kernel, depth), out_shape=[jax.Sha...  223 us
    pallas_call x1, Pallas kernels, run_adamw(): pl.pallas_call(adamw_kernel, out_shape=outs, in_specs=[anywhere] * 2 + [i...  7.88 us

profile of v1, /device:TPU:0, one launch (start us, length us, event | category | flops | bytes accessed | tf_op | source)
XLA Modules:
  0.0 232.6 jit_solution(13634354478502859624)
XLA Ops:
  1.3 223.2 %shard_map.362 = (bf16[1024,768]{1,0:T(8,128)(2,1)}, f32[1024,768]{1,0:T(8,128)}, f32[24,2304]{1,0:T(8,128)}, f32[24,768]{1,0:T(8,128)}, f32[24,3072]{1,0:T(8,12...) custom-call(s32[1,9]{1,0:T(1,128)} %ends_ref.1, s32[1]{0:T(128)S(6)} %copy.42.length_ref, ...), custom_call_target="tpu_custom_call" | custom-call | tf_op jit(solution)/shard_map/pallas_call | solution.py:1650
  224.5 7.9 %shard_map.363 = (bf16[1024,768]{1,0:T(8,128)(2,1)}, f32[1024,768]{1,0:T(8,128)}, f32[1,1]{1,0:T(1,128)}, f32[24,2304]{1,0:T(8,128)}, f32[24,768]{1,0:T(8,128)},...) custom-call(bf16[1024,768]{1,0:T(8,128)(2,1)} %get-tuple-element.54., ...), custom_call_target="tpu_custom_call" | custom-call | tf_op jit(solution)/shard_map/pallas_call | solution.py:1707

commit v2 on v1

--- a/solution.py
+++ b/solution.py
@@ -15,6 +15,7 @@
 BAND = 3 * TILE
 PAIR = 2 * HD
 ROWS = 256
+CHUNK = 32
 
 eps_norm = 1e-06
 far_below = -1000000000.0
@@ -489,6 +490,50 @@
     return jnp.logical_and(left, right)
 
 
+def fold(values):
+    return jnp.sum(values.reshape(-1, 8, values.shape[1]), 0)
+
+
+def chunks_of(count, size):
+    return [slice(start, start + size) for start in range(0, count, size)]
+
+
+def softmax_into(scores, allowed_at, probs):
+    parts = chunks_of(scores.shape[0], 64)
+    top = None
+    for part in parts:
+        value = jnp.where(allowed_at(part), scores[part, :], far_below)
+        scores[part, :] = value
+        high = jnp.max(value.reshape(-1, 8, value.shape[1]), 0)
+        top = high if top is None else jnp.maximum(top, high)
+    top = jnp.max(top, 0, keepdims=True)
+    total = None
+    for part in parts:
+        value = jnp.exp(scores[part, :] - top)
+        scores[part, :] = value
+        total = fold(value) if total is None else total + fold(value)
+    total = jnp.sum(total, 0, keepdims=True)
+    scale = 1.0 / total
+    for part in parts:
+        probs[part, :] = (scores[part, :] * scale).astype(jnp.bfloat16)
+    return top + jnp.log(total)
+
+
+def softmax_back_into(scores, grad_probs, allowed_at, log_total, probs, grad_scores):
+    parts = chunks_of(scores.shape[0], 32)
+    delta = None
+    for part in parts:
+        value = jnp.exp(jnp.where(allowed_at(part), scores[part, :], far_below) - log_total)
+        scores[part, :] = value
+        probs[part, :] = value.astype(jnp.bfloat16)
+        share = fold(value * grad_probs[part, :])
+        delta = share if delta is None else delta + share
+    delta = jnp.sum(delta, 0, keepdims=True)
+    for part in parts:
+        grad = scores[part, :] * (grad_probs[part, :] - delta)
+        grad_scores[part, :] = grad.astype(jnp.bfloat16)
+
+
 class Places:
     def __init__(self, depth):
         self.depth = depth
@@ -731,8 +776,8 @@
     depth, ends_ref, length_ref, wqkv_ref, wout_ref, wup_ref, wdown_ref, vectors_ref, x_hbm, cot_hbm,
     out_hbm, grad_hbm, rqkv_ref, rout_ref, rup_ref, rdown_ref, rvec_ref, norm_ref,
     w, vbuf, vpad, give_out, asm, asm_down, vec, qkv, att, middle, h2, act, du, out_acc, dh2, dy,
-    far, far_got, lse, key_seg, query_seg, turned, h2_tr, flat_up, flat_down,
-    got_a, got_b, got_z, got_zd, red, squares, gvec,
+    far, far_got, lse, key_seg, query_seg, turned, h2_tr, flat_up, flat_down, pre_grad,
+    got_a, got_b, got_z, got_zd, red, squares, gvec, sums_two,
     v_sent, v_got, v_got_z, n_sent, n_got, n_got_z,
     swap_s, swap_r, ag_s, ag_r, vg_s, vg_r, kv_s, kv_r, fg_s, fg_r, rs_s, rs_r, ex_s, ex_r, no_s, no_r, local_s,
 ):
@@ -892,23 +937,42 @@
         whole = whole + jnp.sum(values, 0)
     vec[...] = whole
 
+    def row_chunks(step):
+        return [
+            pl.ds(pl.multiple_of(step * ROWS + start, CHUNK), CHUNK)
+            for start in range(0, ROWS, CHUNK)
+        ]
+
     def first_norm(target, first_time):
         @pl.loop(0, rows // ROWS)
         def _(step):
-            here = rows_at(step)
-            value = dy[here, :].astype(f32)
-            unit, _ = standardize(value)
-            hidden = (unit * vec[0:1, :] + vec[1:2, :]).astype(bf16)
-            if first_time:
-                target[here, :] = hidden
-                middle[here, :] = value
-            else:
-                target[:, here] = hidden.T
+            for here in row_chunks(step):
+                value = dy[here, :].astype(f32)
+                unit, _ = standardize(value)
+                act[here, :] = (unit * vec[0:1, :] + vec[1:2, :]).astype(bf16)
+                if first_time:
+                    middle[here, :] = value
+            if not first_time:
+                target[:, rows_at(step)] = act[rows_at(step), :].T
 
     load_x.wait()
     first_norm(act, True)
     load_dy = pltpu.make_async_copy(cot_hbm, dy, local_s.at[0])
     load_dy.start()
+
+    def allowed_short(tile):
+        start, line = band_start(tile), query_seg[tile]
+
+        def allowed(part):
+            count = part.stop - part.start
+            band = key_seg[pl.ds(pl.multiple_of(start + part.start, 32), count), :]
+            return jnp.concatenate([band, band], 1) == jnp.concatenate([line, line], 1)
+
+        return allowed
+
+    def allowed_long(part):
+        shape = (part.stop - part.start, 2 * TILE)
+        return lax.broadcasted_iota(jnp.int32, shape, 0) + part.start < length_ref[0]
 
     third = 3 * PAIR
 
@@ -1004,10 +1068,11 @@
             att[pair_lanes(group * 2 + side), tile_rows(tile)] = made.astype(bf16)
 
         def soften(tile, side):
-            allowed = short_mask(tile, key_seg, query_seg)
-            probs, log_total = softmax_of(out_acc[slot_rows(side), :wide], allowed)
-            flat_down[slot_rows(side), :wide] = probs
-            lse[tile, group * 2 + side] = log_total
+            lse[tile, group * 2 + side] = softmax_into(
+                out_acc.at[slot_rows(side), :wide],
+                allowed_short(tile),
+                flat_down.at[slot_rows(side), :wide],
+            )
 
         def compare(tile, side):
             queries = stack_heads(qkv[tile_rows(tile), q_at(group, side)], score_scale)
@@ -1046,17 +1111,18 @@
 
     @pl.loop(0, groups)
     def _(group):
-        allowed = long_mask(length_ref, 4 * LONG_DEV)
+        long_rows = lambda side: slice(side * 4 * LONG_DEV, (side + 1) * 4 * LONG_DEV)
+        for side in range(2):
+            queries = stack_heads(qkv[SHORT_DEV:, q_at(group, side)], score_scale)
+            out_acc[long_rows(side), :wide] = dot_tr(far_block(2 * group + side, 0), queries)
         for side in range(2):
             pair = 2 * group + side
-            made, log_total = attend_forward(
-                qkv[SHORT_DEV:, q_at(group, side)],
-                far_block(pair, 0),
-                far_block(pair, PAIR).T,
-                allowed,
+            probs = flat_down.at[: 4 * LONG_DEV, side * wide : (side + 1) * wide]
+            lse[tiles, pair] = softmax_into(
+                out_acc.at[long_rows(side), :wide], allowed_long, probs
             )
-            att[pair_lanes(pair), SHORT_DEV:] = made
-            lse[tiles, pair] = log_total
+            made = unstack_heads(dot(far_block(pair, PAIR).T, probs[...]))
+            att[pair_lanes(pair), SHORT_DEV:] = made.astype(bf16)
         pl.when(group == 0)(lambda: gather_even(3 * groups + 1))
         pl.when(group == groups - 1)(lambda: gather_odd(3 * groups + 1))
 
@@ -1082,11 +1148,10 @@
 
     @pl.loop(0, rows // ROWS)
     def _(step):
-        here = rows_at(step)
-        unit, _ = standardize(middle[here, :])
-        hidden = (unit * vec[2:3, :] + vec[3:4, :]).astype(bf16)
-        h2[here, :] = hidden
-        h2_tr[:, here] = hidden.T
+        for here in row_chunks(step):
+            unit, _ = standardize(middle[here, :])
+            h2[here, :] = (unit * vec[2:3, :] + vec[3:4, :]).astype(bf16)
+        h2_tr[:, rows_at(step)] = h2[rows_at(step), :].T
 
     def piece(block, place):
         return w.at[block, at.c, place]
@@ -1283,13 +1348,19 @@
                 scatter_pump(4 * unit + 1)
 
             columns = wide_at(step)
-            pre = dot(h2[...], flat_up[:, columns]) + vec[pl.ds(8 + unit, 1), columns]
-            grad_act = dot_tr(dy[...], flat_down[columns, :])
-            made, slope = gelu_both(pre)
-            act[:, columns] = made.astype(bf16)
-            du_low = (grad_act * slope).astype(bf16)
-            du[:, columns] = du_low
-            gvec[pl.ds(8 + unit, 1), columns] = column_sum(du_low.astype(f32))
+            bias = vec[pl.ds(8 + unit, 1), columns]
+            total = jnp.zeros((8, wide), f32)
+            for half_rows in chunks_of(rows, rows // 2):
+                pre_grad[:, :wide] = dot(h2[half_rows, :], flat_up[:, columns])
+                pre_grad[:, wide:] = dot_tr(dy[half_rows, :], flat_down[columns, :])
+                for part in chunks_of(rows // 2, CHUNK):
+                    here = slice(half_rows.start + part.start, half_rows.start + part.stop)
+                    made, slope = gelu_both(pre_grad[part, :wide] + bias)
+                    act[here, columns] = made.astype(bf16)
+                    du_low = (pre_grad[part, wide:] * slope).astype(bf16)
+                    du[here, columns] = du_low
+                    total = total + fold(du_low.astype(f32))
+            gvec[pl.ds(8 + unit, 1), columns] = column_sum(total)
 
         @pl.loop(0, width // wide)
         def _(step):
@@ -1307,29 +1378,30 @@
         give(up, dot(h2_tr[...], du[...]))
         give(down, dot_tl(act[...], dy[...]), True)
 
-    def body(step, totals):
-        here = rows_at(step)
+    sums_two[...] = jnp.zeros_like(sums_two)
+
+    @pl.loop(0, rows // ROWS)
+    def _(step):
         for turn in range(rows // ROWS):
             pl.when(step == turn)(functools.partial(scatter_pump, 4 * units + turn))
-        middle_here = middle[here, :]
-        out = middle_here + (out_acc[here, :] + vec[7:8, :])
-        h2[here, :] = out.astype(bf16)
-        dy_here = dy[here, :].astype(f32)
-        dh2_here = dh2[here, :]
-        unit, inv_std = standardize(middle_here)
-        dmiddle = dy_here + norm_back(dh2_here, unit, inv_std, vec[2:3, :])
-        dh2[here, :] = dmiddle
-        da = dmiddle.astype(bf16)
-        act[here, :] = da
-        return (
-            totals[0] + column_sum(dh2_here * unit),
-            totals[1] + column_sum(dh2_here),
-            totals[2] + column_sum(da.astype(f32)),
-            totals[3] + column_sum(dy_here),
-        )
-
-    zero = jnp.zeros((1, width), f32)
-    sums = lax.fori_loop(0, rows // ROWS, body, (zero,) * 4)
+        for here in row_chunks(step):
+            middle_here = middle[here, :]
+            out = middle_here + (out_acc[here, :] + vec[7:8, :])
+            h2[here, :] = out.astype(bf16)
+            dy_here = dy[here, :].astype(f32)
+            dh2_here = dh2[here, :]
+            unit, inv_std = standardize(middle_here)
+            dmiddle = dy_here + norm_back(dh2_here, unit, inv_std, vec[2:3, :])
+            dh2[here, :] = dmiddle
+            da = dmiddle.astype(bf16)
+            act[here, :] = da
+            sums_two[0] += fold(dh2_here * unit)
+            sums_two[1] += fold(dh2_here)
+            sums_two[2] += fold(da.astype(f32))
+            sums_two[3] += fold(dy_here)
+
+    for place, line in enumerate((2, 3, 6, 7)):
+        gvec[line : line + 1, :] = column_sum(sums_two[place])
     flatten(flat_up, groups)
 
     @pl.loop(0, width // wide)
@@ -1337,8 +1409,6 @@
         columns = wide_at(step)
         du[:, columns] = dot_tr(act[...], flat_up[columns, :]).astype(bf16)
 
-    for place, total in zip((2, 3, 6, 7), sums):
-        gvec[place : place + 1, :] = total
     store_out = pltpu.make_async_copy(h2, out_hbm, local_s.at[0])
     store_out.start()
     load_again = pltpu.make_async_copy(x_hbm, dy, local_s.at[2])
@@ -1351,19 +1421,32 @@
 
     @pl.loop(0, groups)
     def _(group):
-        allowed = long_mask(length_ref, 4 * LONG_DEV)
+        long_rows = lambda side: slice(side * 4 * LONG_DEV, (side + 1) * 4 * LONG_DEV)
+
+        def stacked_long(side):
+            return (
+                stack_heads(qkv[SHORT_DEV:, q_at(group, side)], score_scale),
+                stack_heads(du[SHORT_DEV:, pair_lanes(2 * group + side)], None),
+            )
+
         for side in range(2):
-            pair = 2 * group + side
-            dq, dk, dv = attend_back(
-                qkv[SHORT_DEV:, q_at(group, side)],
-                far_block(pair, 0),
-                far_block(pair, 0).T,
-                far_block(pair, PAIR),
-                allowed,
-                lse[tiles, pair],
-                du[SHORT_DEV:, pair_lanes(pair)],
+            queries, upstream = stacked_long(side)
+            here, pair = long_rows(side), 2 * group + side
+            out_acc[here, :wide] = dot_tr(far_block(pair, 0), queries)
+            out_acc[here, wide : 2 * wide] = dot_tr(far_block(pair, PAIR), upstream)
+        for side in range(2):
+            queries, upstream = stacked_long(side)
+            here, pair = long_rows(side), 2 * group + side
+            lanes = slice(side * wide, (side + 1) * wide)
+            probs = flat_down.at[: 4 * LONG_DEV, lanes]
+            grad_scores = flat_up.at[: 4 * LONG_DEV, lanes]
+            softmax_back_into(
+                out_acc.at[here, :wide], out_acc.at[here, wide : 2 * wide], allowed_long,
+                lse[tiles, pair], probs, grad_scores,
             )
-            qkv[SHORT_DEV:, q_at(group, side)] = dq
+            dk, dv = dot(grad_scores[...], queries), dot(probs[...], upstream)
+            dq = unstack_heads(dot(far_block(pair, 0).T, grad_scores[...])) * score_scale
+            qkv[SHORT_DEV:, q_at(group, side)] = dq.astype(bf16).T
             far[:, :, far_pair(pair, 0)] = dk.astype(bf16).reshape(4, LONG_DEV, PAIR)
             far[:, :, far_pair(pair, PAIR)] = dv.astype(bf16).reshape(4, LONG_DEV, PAIR)
         for turn in range(groups):
@@ -1433,15 +1516,14 @@
             h2[tile_rows(target), pair_lanes(group * 2 + side)] = dq.astype(bf16).T
 
         def soften(tile, side, source):
-            allowed = short_mask(tile, key_seg, query_seg)
-            probs, grad_scores = softmax_back(
-                middle[slot_rows(side), 2 * wide : 3 * wide],
-                allowed,
+            softmax_back_into(
+                middle.at[slot_rows(side), 2 * wide : 3 * wide],
+                out_acc.at[slot_rows(side), :wide],
+                allowed_short(tile),
                 lse[source, group * 2 + side],
-                out_acc[slot_rows(side), :wide],
+                flat_down.at[slot_rows(side), :wide],
+                flat_down.at[slot_rows(side), wide : 2 * wide],
             )
-            flat_down[slot_rows(side), :wide] = probs
-            flat_down[slot_rows(side), wide : 2 * wide] = grad_scores
 
         def compare(tile, side):
             queries, upstream = stacked(tile, side)
@@ -1508,11 +1590,18 @@
                 gvec[line : line + 1, own] = sums[:, lane : lane + PAIR]
 
     def input_rows(step):
-        here = pl.ds(step * (rows // 2), rows // 2)
-        unit, inv_std = standardize(dy[here, :].astype(f32))
-        dh1 = out_acc[here, :]
-        middle[here, :] = dh2[here, :] + norm_back(dh1, unit, inv_std, vec[0:1, :])
-        return column_sum(dh1 * unit), column_sum(dh1)
+        sums_two[0:2] = jnp.zeros((2, 8, width), f32)
+
+        @pl.loop(step * (rows // ROWS // 2), (step + 1) * (rows // ROWS // 2))
+        def _(block):
+            for here in row_chunks(block):
+                unit, inv_std = standardize(dy[here, :].astype(f32))
+                dh1 = out_acc[here, :]
+                middle[here, :] = dh2[here, :] + norm_back(dh1, unit, inv_std, vec[0:1, :])
+                sums_two[0] += fold(dh1 * unit)
+                sums_two[1] += fold(dh1)
+
+        return column_sum(sums_two[0]), column_sum(sums_two[1])
 
     latest = groups - 1
     scatter_one(latest)
@@ -1627,6 +1716,7 @@
         vmem((width, rows), bf16),
         vmem((width, width), bf16),
         vmem((width, width), bf16),
+        vmem((rows // 2, 4 * PAIR), f32),
         vmem((blocks, 2, depth, slab, half), bf16),
         vmem((blocks, depth, slab, half), bf16),
         vmem((blocks, depth - 1, slab, half), bf16),
@@ -1634,6 +1724,7 @@
         vmem((slots * share + tall, width), f32),
         vmem((slab, half), f32),
         vmem((16, width), f32),
+        vmem((4, 8, width), f32),
         vmem((4, 16, width), f32),
         vmem((3, 16, width), f32),
         vmem((depth, 16, width), f32),

time: 233 us -> 233 us (level)
  no operation moved by 1% of the time
where the time goes in v2:
time: 233 us
  Pallas kernels  231 us (99%)
    pallas_call x1, Pallas kernels, run_fused(): pl.pallas_call(functools.partial(fused_kernel, depth), out_shape=[jax.Sha...  224 us
    pallas_call x1, Pallas kernels, run_adamw(): pl.pallas_call(adamw_kernel, out_shape=outs, in_specs=[anywhere] * 2 + [i...  7.88 us

profile of v2, /device:TPU:0, one launch (start us, length us, event | category | flops | bytes accessed | tf_op | source)
XLA Modules:
  0.0 232.9 jit_solution(9366237194572285051)
XLA Ops:
  1.3 223.5 %shard_map.362 = (bf16[1024,768]{1,0:T(8,128)(2,1)}, f32[1024,768]{1,0:T(8,128)}, f32[24,2304]{1,0:T(8,128)}, f32[24,768]{1,0:T(8,128)}, f32[24,3072]{1,0:T(8,12...) custom-call(s32[1,9]{1,0:T(1,128)} %ends_ref.1, s32[1]{0:T(128)S(6)} %copy.42.length_ref, ...), custom_call_target="tpu_custom_call" | custom-call | tf_op jit(solution)/shard_map/pallas_call | solution.py:1741
  224.9 7.9 %shard_map.363 = (bf16[1024,768]{1,0:T(8,128)(2,1)}, f32[1024,768]{1,0:T(8,128)}, f32[1,1]{1,0:T(1,128)}, f32[24,2304]{1,0:T(8,128)}, f32[24,768]{1,0:T(8,128)},...) custom-call(bf16[1024,768]{1,0:T(8,128)(2,1)} %get-tuple-element.54., ...), custom_call_target="tpu_custom_call" | custom-call | tf_op jit(solution)/shard_map/pallas_call | solution.py:1798

commit v3 on v2

--- a/solution.py
+++ b/solution.py
@@ -891,7 +891,11 @@
         last, block = turn - 3, turn
         when(both(last >= 0, last < blocks), lambda: weights.stage_four(last))
 
-        when(block < blocks, lambda: weights.stage_two(block))
+        def second():
+            weights.stage_two(block)
+            when(block + groups < blocks, lambda: push(block + groups))
+
+        when(block < blocks, second)
 
     def gather_odd(turn):
         block = turn - 1
@@ -906,13 +910,9 @@
     swaps[2].wait_recv()
     vectors.stage_two(0)
     gather_even(0)
-    for block in range(groups, 2 * groups):
-        push(block)
     vectors.stage_three(0)
     gather_even(1)
     gather_odd(1)
-    for block in range(2 * groups, blocks):
-        push(block)
     vectors.stage_four(0)
     gather_even(2)
     gather_odd(2)
@@ -1477,14 +1477,14 @@
             @pl.when(group > 0)
             def _():
                 if place == 0:
+                    pl.when(group > 1)(lambda: scatter_three(group - 2))
+                if place == 2:
                     pl.when(group > 1)(lambda: scatter_four(group - 2))
                 if place == 1:
                     for block in range(groups - 1):
                         pl.when(before == block)(functools.partial(scatter_one, block))
                 if place == 3:
                     scatter_two(before)
-                if place == 4:
-                    scatter_three(before)
 
         pump(0)
         for side in range(2):
@@ -1604,6 +1604,7 @@
         return column_sum(sums_two[0]), column_sum(sums_two[1])
 
     latest = groups - 1
+    scatter_three(latest - 1)
     scatter_one(latest)
 
     @pl.loop(0, width // wide)

time: 233 us -> 228 us (0.979)
  Pallas kernels: 231 us -> 227 us
    pallas_call x1, Pallas kernels: 224 us -> 219 us  [run_fused(): pl.pallas_call(functools.partial(fused_kernel, depth), out_shape=[jax.Sha...]
where the time goes in v3:
time: 228 us
  Pallas kernels  227 us (100%)
    pallas_call x1, Pallas kernels, run_fused(): pl.pallas_call(functools.partial(fused_kernel, depth), out_shape=[jax.Sha...  219 us
    pallas_call x1, Pallas kernels, run_adamw(): pl.pallas_call(adamw_kernel, out_shape=outs, in_specs=[anywhere] * 2 + [i...  7.88 us

profile of v3, /device:TPU:0, one launch (start us, length us, event | category | flops | bytes accessed | tf_op | source)
XLA Modules:
  0.0 228.3 jit_solution(3620362466612163890)
XLA Ops:
  1.3 218.9 %shard_map.362 = (bf16[1024,768]{1,0:T(8,128)(2,1)}, f32[1024,768]{1,0:T(8,128)}, f32[24,2304]{1,0:T(8,128)}, f32[24,768]{1,0:T(8,128)}, f32[24,3072]{1,0:T(8,12...) custom-call(s32[1,9]{1,0:T(1,128)} %ends_ref.1, s32[1]{0:T(128)S(6)} %copy.42.length_ref, ...), custom_call_target="tpu_custom_call" | custom-call | tf_op jit(solution)/shard_map/pallas_call | solution.py:1742
  220.2 7.9 %shard_map.363 = (bf16[1024,768]{1,0:T(8,128)(2,1)}, f32[1024,768]{1,0:T(8,128)}, f32[1,1]{1,0:T(1,128)}, f32[24,2304]{1,0:T(8,128)}, f32[24,768]{1,0:T(8,128)},...) custom-call(bf16[1024,768]{1,0:T(8,128)(2,1)} %get-tuple-element.54., ...), custom_call_target="tpu_custom_call" | custom-call | tf_op jit(solution)/shard_map/pallas_call | solution.py:1799
